TPU v7x, 256 devices: a whole 4x4x8 slice. The times are simulated.
256 devices in a mesh: dp: 8 (over y, x_hi), tok: 8 (over z), hid: 4 (over x_lo, core).
Axes of the slice: x: 4 (x_hi: 2, x_lo: 2; x = x_hi * 2 + x_lo), y: 4, z: 8, core: 2. Of those that a mesh axis runs over, the one named last changes fastest.
Arguments:
- tokens: bfloat16 [8192, 3072], P(('dp', 'tok'), 'hid'), may hold values from -40 to 40
- w_in: bfloat16 [3072, 12288], P('hid', 'tok'), may hold values from -0.108253175 to 0.108253175
- w_out: bfloat16 [12288, 3072], P('tok', 'hid'), may hold values from -0.0546875 to 0.0546875
- gain: float32 [3072], P('hid'), may hold values from 0.2 to 4, as said below
- cotangent: bfloat16 [8192, 3072], P(('dp', 'tok'), 'hid'), may hold values from -6 to 6
Outputs:
- mixed: bfloat16 [8192, 3072], P(('dp', 'tok'), 'hid')
- grad_input: bfloat16 [8192, 3072], P(('dp', 'tok'), 'hid')
- grad_w_in: bfloat16 [3072, 12288], P('hid', 'tok')
- grad_w_out: bfloat16 [12288, 3072], P('tok', 'hid')
Inputs may be any that keep to these rules, and one draw needn't show every extreme that they name: `gain`: positive.
All inputs are finite; a program needn't handle non-finite values.
Results may differ from a plain program's by a relative error of at most 0.024.
Values may be sent and summed in bfloat16 or wider, within the bound.
A program may use at most 128 MiB of HBM per device.

v0:
```python
import math

import jax
import jax.numpy as jnp
from jax import lax
from jax.sharding import PartitionSpec as P

D = 3072


norm_eps = 1e-06


def gelu_pair(pre_act):
    cdf_part = 0.5 * (1.0 + jax.scipy.special.erf(pre_act * (1.0 / math.sqrt(2.0))))
    dens_part = jnp.exp(-0.5 * pre_act * pre_act) * (1.0 / math.sqrt(2.0 * math.pi))
    return (pre_act * cdf_part, cdf_part + pre_act * dens_part)


def right_contract(left_op, right_op):
    return lax.dot_general(
        left_op, right_op, (((1,), (1,)), ((), ())), preferred_element_type=jnp.float32
    )


def row_contract(left_op, right_op):
    return lax.dot_general(
        left_op, right_op, (((0,), (0,)), ((), ())), preferred_element_type=jnp.float32
    )


def shards(tokens, w_in, w_out, gain, cotangent):
    tok_rows = tokens.shape[0]
    n_tok = lax.axis_size("tok")
    grad_scale = 1.0 / math.sqrt(tok_rows * n_tok * lax.axis_size("dp"))
    tok_float = tokens.astype(jnp.float32)
    row_sums, squares = lax.psum(
        (jnp.sum(tok_float, axis=1), jnp.sum(tok_float * tok_float, axis=1)), "hid"
    )
    row_mean = (row_sums / D)[:, None]
    row_rstd = lax.rsqrt(squares[:, None] / D - row_mean * row_mean + norm_eps)
    centred = (tok_float - row_mean) * row_rstd
    normed = (centred * gain[None, :]).astype(jnp.bfloat16)
    gathered = lax.all_gather(normed, "tok", axis=0, tiled=True)
    pre_act = lax.psum_scatter(
        jnp.dot(gathered, w_in, preferred_element_type=jnp.float32).astype(jnp.bfloat16),
        "hid",
        scatter_dimension=0,
        tiled=True,
    ).astype(jnp.float32)
    act_share, slopes = gelu_pair(pre_act)
    hidden = lax.all_gather(act_share.astype(jnp.bfloat16), "hid", axis=0, tiled=True)
    branch = lax.psum_scatter(
        jnp.dot(hidden, w_out, preferred_element_type=jnp.float32).astype(jnp.bfloat16),
        "tok",
        scatter_dimension=0,
        tiled=True,
    ).astype(jnp.float32)
    mixed = (tok_float + branch).astype(jnp.bfloat16)
    cot_group = lax.all_gather(cotangent, "tok", axis=0, tiled=True)
    out_local = row_contract(hidden, cot_group) * grad_scale
    grad_act = lax.psum_scatter(
        right_contract(cot_group, w_out).astype(jnp.bfloat16),
        "hid",
        scatter_dimension=0,
        tiled=True,
    ).astype(jnp.float32)
    grad_share = (grad_act * slopes).astype(jnp.bfloat16)
    grad_hidden = lax.all_gather(grad_share, "hid", axis=0, tiled=True)
    grad_normed = lax.psum_scatter(
        right_contract(grad_hidden, w_in).astype(jnp.bfloat16),
        "tok",
        scatter_dimension=0,
        tiled=True,
    ).astype(jnp.float32)
    grad_scaled = grad_normed * gain[None, :]
    first_sum, second_sum = lax.psum(
        (jnp.sum(grad_scaled, axis=1), jnp.sum(grad_scaled * centred, axis=1)), "hid"
    )
    first_mean = (first_sum / D)[:, None]
    second_mean = (second_sum / D)[:, None]
    grad_input = (
        cotangent.astype(jnp.float32)
        + row_rstd * (grad_scaled - first_mean - centred * second_mean)
    ).astype(jnp.bfloat16)
    in_local = row_contract(gathered, grad_hidden) * grad_scale
    in_summed, out_summed = (
        lax.psum_scatter(
            in_local.astype(jnp.bfloat16), "dp", scatter_dimension=0, tiled=True
        ).astype(jnp.float32),
        lax.psum_scatter(
            out_local.astype(jnp.bfloat16), "dp", scatter_dimension=0, tiled=True
        ).astype(jnp.float32),
    )
    grad_w_in, grad_w_out = (
        lax.all_gather(in_summed.astype(jnp.bfloat16), "dp", axis=0, tiled=True),
        lax.all_gather(out_summed.astype(jnp.bfloat16), "dp", axis=0, tiled=True),
    )
    return (mixed, grad_input, grad_w_in, grad_w_out)


def solution(mesh):
    in_specs = (
        P(("dp", "tok"), "hid"),
        P("hid", "tok"),
        P("tok", "hid"),
        P("hid"),
        P(("dp", "tok"), "hid"),
    )
    out_specs = (P(("dp", "tok"), "hid"), P(("dp", "tok"), "hid"), P("hid", "tok"), P("tok", "hid"))
    return jax.shard_map(shards, mesh=mesh, in_specs=in_specs, out_specs=out_specs, check_vma=False)
```

profile of v0, /device:TPU:1, one launch (start us, length us, event | category | flops | bytes accessed | tf_op | source)
XLA Modules:
  0.0 662.8 jit_solution(10016810541559797207)
XLA Ops:
  7.2 0.0 copy-start
  7.2 0.0 all-gather.7.cloned.1.call-start
  7.2 1.2 convert_reduce_fusion
  8.4 8.3 %all-reduce.1 = (f32[128]{0:T(128)S(1)}, f32[128]{0:T(128)S(1)}) all-reduce(f32[128]{0:T(128)S(1)} %get-tuple-element.7, f32[128]{0:T(128)S(1)} %get-tuple-element.6), channel_id=1, replica_groups=mesh['dp'=8,'tok'=8,'hid'=4] {'hid'}, use_global_device_ids=true, to_apply=%region_3.0 | all-reduce | flops 256 | bytes 2048 | tf_op jit(solution)/shard_map/psum | solution.py:37
  16.7 1.8 fusion.13
  18.5 0.0 all-gather.7.cloned.1.call-update
  18.5 0.0 all-gather.11.cloned.1.call-start
  18.6 0.7 all-gather.11.cloned.1.call-update
  19.3 0.0 reduce-scatter.7.cloned.1.call-start
  19.3 37.6 %all-gather.7.cloned.1.call-done = bf16[1024,768]{1,0:T(8,128)(2,1)} async-done(((bf16[128,768]{1,0:T(8,128)(2,1)}), bf16[1024,768]{1,0:T(8,128)(2,1)}) %all-gather.7.cloned.1.call-update) | async-done | bytes 1572880 | tf_op jit(solution)/shard_map/all_gather | solution.py:44
  57.0 0.0 copy-done
  57.0 5.4 convolution_convert_fusion.1
  62.4 0.0 reduce-scatter.7.cloned.1.call-update
  62.4 0.0 reduce-scatter.11.cloned.1.call-start
  62.5 34.9 %all-gather.11.cloned.1.call-done = bf16[1024,768]{1,0:T(8,128)(2,1)} async-done(((bf16[128,768]{1,0:T(8,128)(2,1)}), bf16[1024,768]{1,0:T(8,128)(2,1)}) %all-gather.11.cloned.1.call-update) | async-done | bytes 1572880 | tf_op jit(solution)/shard_map/all_gather | solution.py:60
  97.4 6.4 convolution_convert_fusion
  103.8 0.0 reduce-scatter.11.cloned.1.call-update
  103.8 0.0 all-gather.9.cloned.1.call-start
  103.9 38.1 %reduce-scatter.7.cloned.1.call-done = bf16[256,1536]{1,0:T(8,128)(2,1)} async-done(((bf16[1024,1536]{1,0:T(8,128)(2,1)}), bf16[256,1536]{1,0:T(8,128)(2,1)}) %reduce-scatter.7.cloned.1.call-update) | async-done | bytes 786448 | tf_op jit(solution)/shard_map/reduce_scatter | solution.py:45
  142.0 42.8 %reduce-scatter.11.cloned.1.call-done = bf16[256,1536]{1,0:T(8,128)(2,1)} async-done(((bf16[1024,1536]{1,0:T(8,128)(2,1)}), bf16[256,1536]{1,0:T(8,128)(2,1)}) %reduce-scatter.11.cloned.1.call-update) | async-done | bytes 786448 | tf_op jit(solution)/shard_map/reduce_scatter | solution.py:62
  184.7 3.3 fusion.8
  188.1 0.0 all-gather.9.cloned.1.call-update
  188.1 0.0 all-gather.13.cloned.1.call-start
  188.1 0.5 all-gather.13.cloned.1.call-update
  188.7 0.0 reduce-scatter.17.cloned.1.call-start
  188.7 41.0 %all-gather.9.cloned.1.call-done = bf16[1024,1536]{1,0:T(8,128)(2,1)} async-done(((bf16[256,1536]{1,0:T(8,128)(2,1)}), bf16[1024,1536]{1,0:T(8,128)(2,1)}) %all-gather.9.cloned.1.call-update) | async-done | bytes 3145744 | tf_op jit(solution)/shard_map/all_gather | solution.py:52
  229.8 6.4 multiply_convert_fusion
  236.2 0.0 reduce-scatter.17.cloned.1.call-update
  236.2 0.0 reduce-scatter.15.cloned.1.call-start
  236.3 37.0 %all-gather.13.cloned.1.call-done = bf16[1024,1536]{1,0:T(8,128)(2,1)} async-done(((bf16[256,1536]{1,0:T(8,128)(2,1)}), bf16[1024,1536]{1,0:T(8,128)(2,1)}) %all-gather.13.cloned.1.call-update) | async-done | bytes 3145744 | tf_op jit(solution)/shard_map/all_gather | solution.py:69
  273.3 6.4 multiply_convert_fusion.1
  279.7 0.0 reduce-scatter.15.cloned.1.call-update
  279.7 0.0 reduce-scatter.13.cloned.1.call-start
  279.8 5.7 convolution_convert_fusion.2
  285.5 0.0 reduce-scatter.13.cloned.1.call-update
  285.5 0.0 copy-start.1
  285.5 0.0 copy-start.4
  285.5 0.2 reduce-scatter.9.cloned.1.call-start
  285.7 6.4 convolution_convert_fusion.3
  292.1 0.0 copy-start.3
  292.1 0.0 reduce-scatter.9.cloned.1.call-update
  292.2 0.0 all-gather.17.cloned.1.call-start
  292.2 66.3 %reduce-scatter.17.cloned.1.call-done = bf16[192,768]{1,0:T(8,128)(2,1)} async-done(((bf16[1536,768]{1,0:T(8,128)(2,1)}), bf16[192,768]{1,0:T(8,128)(2,1)}) %reduce-scatter.17.cloned.1.call-update) | async-done | bytes 294928 | tf_op jit(solution)/shard_map/reduce_scatter | solution.py:91
  358.5 0.0 all-gather.17.cloned.1.call-update
  358.5 0.0 all-gather.15.cloned.1.call-start
  358.6 84.7 %reduce-scatter.15.cloned.1.call-done = bf16[96,1536]{1,0:T(8,128)(2,1)} async-done(((bf16[768,1536]{1,0:T(8,128)(2,1)}), bf16[96,1536]{1,0:T(8,128)(2,1)}) %reduce-scatter.15.cloned.1.call-update) | async-done | bytes 294928 | tf_op jit(solution)/shard_map/reduce_scatter | solution.py:88
  443.3 0.0 all-gather.15.cloned.1.call-update
  443.3 39.1 %reduce-scatter.13.cloned.1.call-done = bf16[128,768]{1,0:T(8,128)(2,1)} async-done(((bf16[1024,768]{1,0:T(8,128)(2,1)}), bf16[128,768]{1,0:T(8,128)(2,1)}) %reduce-scatter.13.cloned.1.call-update) | async-done | bytes 196624 | tf_op jit(solution)/shard_map/reduce_scatter | solution.py:70
  482.5 0.0 copy-done.1
  482.5 0.0 copy-done.4
  482.5 1.1 fusion.21
  483.6 9.7 %all-reduce = (f32[128]{0:T(128)S(1)}, f32[128]{0:T(128)S(1)}) all-reduce(f32[128]{0:T(128)S(1)} %get-tuple-element.5, f32[128]{0:T(128)S(1)} %get-tuple-element.4), channel_id=1, replica_groups=mesh['dp'=8,'tok'=8,'hid'=4] {'hid'}, use_global_device_ids=true, to_apply=%region_11.0 | all-reduce | flops 256 | bytes 2048 | tf_op jit(solution)/shard_map/psum | solution.py:77
  493.3 30.6 %reduce-scatter.9.cloned.1.call-done = bf16[128,768]{1,0:T(8,128)(2,1)} async-done(((bf16[1024,768]{1,0:T(8,128)(2,1)}), bf16[128,768]{1,0:T(8,128)(2,1)}) %reduce-scatter.9.cloned.1.call-update) | async-done | bytes 196624 | tf_op jit(solution)/shard_map/reduce_scatter | solution.py:53
  523.9 0.0 copy-done.3
  523.9 2.0 fusion.18
  525.8 63.9 %all-gather.17.cloned.1.call-done = bf16[1536,768]{1,0:T(8,128)(2,1)} async-done(((bf16[192,768]{1,0:T(8,128)(2,1)}), bf16[1536,768]{1,0:T(8,128)(2,1)}) %all-gather.17.cloned.1.call-update) | async-done | bytes 2359312 | tf_op jit(solution)/shard_map/all_gather | solution.py:97
  589.7 61.5 %all-gather.15.cloned.1.call-done = bf16[768,1536]{1,0:T(8,128)(2,1)} async-done(((bf16[96,1536]{1,0:T(8,128)(2,1)}), bf16[768,1536]{1,0:T(8,128)(2,1)}) %all-gather.15.cloned.1.call-update) | async-done | bytes 2359312 | tf_op jit(solution)/shard_map/all_gather | solution.py:96
  651.2 0.0 copy-start.2
  651.2 3.4 copy.11
  654.6 0.0 copy-done.2
  654.6 1.4 copy.12
  (2 shorter events, 0.0 us)
Async XLA Ops:
  7.2 49.8 %copy-start = (bf16[768,1536]{1,0:T(8,128)(2,1)S(1)}, bf16[768,1536]{1,0:T(8,128)(2,1)}, u32[]{:S(2)}) copy-start(bf16[768,1536]{1,0:T(8,128)(2,1)} %param.6) | copy-start | bytes 7077892
  7.2 49.8 %all-gather.7.cloned.1.call-start = ((), (), s32[]{:S(2)}) async-start(), calls=%async_computation.6 | async-start | bytes 1769472 | tf_op jit(solution)/shard_map/all_gather | solution.py:44
  18.5 78.9 %all-gather.11.cloned.1.call-start = ((), (), s32[]{:S(2)}) async-start(), calls=%async_computation.10 | async-start | bytes 1769472 | tf_op jit(solution)/shard_map/all_gather | solution.py:60
  19.3 122.7 %reduce-scatter.7.cloned.1.call-start = ((), (), s32[]{:S(2)}) async-start(), calls=%async_computation.7 | async-start | bytes 3932160 | tf_op jit(solution)/shard_map/reduce_scatter | solution.py:45
  62.4 122.3 %reduce-scatter.11.cloned.1.call-start = ((), (), s32[]{:S(2)}) async-start(), calls=%async_computation.11 | async-start | bytes 3932160 | tf_op jit(solution)/shard_map/reduce_scatter | solution.py:62
  103.8 125.9 %all-gather.9.cloned.1.call-start = ((), (), s32[]{:S(2)}) async-start(), calls=%async_computation.8 | async-start | bytes 3932160 | tf_op jit(solution)/shard_map/all_gather | solution.py:52
  188.1 85.2 %all-gather.13.cloned.1.call-start = ((), (), s32[]{:S(2)}) async-start(), calls=%async_computation.12 | async-start | bytes 3932160 | tf_op jit(solution)/shard_map/all_gather | solution.py:69
  188.7 169.8 %reduce-scatter.17.cloned.1.call-start = ((), (), s32[]{:S(2)}) async-start(), calls=%async_computation.16 | async-start | bytes 2654208 | tf_op jit(solution)/shard_map/reduce_scatter | solution.py:91
  236.2 207.1 %reduce-scatter.15.cloned.1.call-start = ((), (), s32[]{:S(2)}) async-start(), calls=%async_computation.14 | async-start | bytes 2654208 | tf_op jit(solution)/shard_map/reduce_scatter | solution.py:88
  279.7 202.7 %reduce-scatter.13.cloned.1.call-start = ((), (), s32[]{:S(2)}) async-start(), calls=%async_computation.13 | async-start | bytes 1769472 | tf_op jit(solution)/shard_map/reduce_scatter | solution.py:70
  285.5 197.0 %copy-start.1 = (bf16[128,768]{1,0:T(8,128)(2,1)S(1)}, bf16[128,768]{1,0:T(8,128)(2,1)}, u32[]{:S(2)}) copy-start(bf16[128,768]{1,0:T(8,128)(2,1)} %param.5) | copy-start | bytes 589828
  285.5 197.0 %copy-start.4 = (f32[768]{0:T(1024)S(1)}, f32[768]{0:T(1024)}, u32[]{:S(2)}) copy-start(f32[768]{0:T(1024)} %param.8) | copy-start | bytes 9220
  285.5 238.4 %reduce-scatter.9.cloned.1.call-start = ((), (), s32[]{:S(2)}) async-start(), calls=%async_computation.9 | async-start | bytes 1769472 | tf_op jit(solution)/shard_map/reduce_scatter | solution.py:53
  292.1 231.7 %copy-start.3 = (bf16[128,768]{1,0:T(8,128)(2,1)S(1)}, bf16[128,768]{1,0:T(8,128)(2,1)}, u32[]{:S(2)}) copy-start(bf16[128,768]{1,0:T(8,128)(2,1)} %param.9) | copy-start | bytes 589828
  292.2 297.6 %all-gather.17.cloned.1.call-start = ((), (), s32[]{:S(2)}) async-start(), calls=%async_computation.17 | async-start | bytes 2654208 | tf_op jit(solution)/shard_map/all_gather | solution.py:97
  358.5 292.7 %all-gather.15.cloned.1.call-start = ((), (), s32[]{:S(2)}) async-start(), calls=%async_computation.15 | async-start | bytes 2654208 | tf_op jit(solution)/shard_map/all_gather | solution.py:96
  651.2 3.4 copy-start.2
Sparse Core Ops, SparseCore 0:
  18.6 38.2 all-gather.6
  58.7 38.5 all-gather.10
  99.9 42.0 reduce-scatter.6
  144.4 40.3 reduce-scatter.10
  188.2 41.4 all-gather.8
  232.0 41.2 all-gather.12
  277.9 80.5 reduce-scatter.16
  363.1 80.1 reduce-scatter.14
  445.9 36.5 reduce-scatter.12
  484.9 38.9 reduce-scatter.8
  526.5 63.2 all-gather.16
  592.2 58.9 all-gather.14
where the time goes:
time: 663 us
  waiting for transfers between devices  579 us (87%)
  matrix products  36.8 us (6%)
  blocking collectives  18 us (3%)
  between operations  14.2 us (2%)
  other arithmetic  9.42 us (1%)
    reduce_scatter x1, waiting for transfers between devices, shards(): lax.psum_scatter(in_local.astype(jnp.bfloat16), 'dp', scatter_dimension=0...  84.7 us
    reduce_scatter x1, waiting for transfers between devices, shards(): lax.psum_scatter(out_local.astype(jnp.bfloat16), 'dp', scatter_dimension=...  66.3 us
    all_gather x1, waiting for transfers between devices, shards(): lax.all_gather(out_summed.astype(jnp.bfloat16), 'dp', axis=0, tiled=True)  63.9 us
    all_gather x1, waiting for transfers between devices, shards(): lax.all_gather(in_summed.astype(jnp.bfloat16), 'dp', axis=0, tiled=True)  61.5 us
    reduce_scatter x1, waiting for transfers between devices, shards(): lax.psum_scatter(right_contract(cot_group, w_out).astype(jnp.bfloat16), '...  42.8 us
    all_gather x1, waiting for transfers between devices, shards(): lax.all_gather(act_share.astype(jnp.bfloat16), 'hid', axis=0, tiled=True)  41 us
    reduce_scatter x1, waiting for transfers between devices, shards(): lax.psum_scatter(right_contract(grad_hidden, w_in).astype(jnp.bfloat16),...  39.1 us
    reduce_scatter x1, waiting for transfers between devices, shards(): lax.psum_scatter(jnp.dot(gathered, w_in, preferred_element_type=jnp.float...  38.1 us
  transfers between devices with their start and end apart: 12, of which 12 were waited for; matrix products, arithmetic and copies ran while one was open for 6% of the time, Pallas kernels for 0%

commit v1 on v0

v1 whole, which is shorter than its diff:
```python
import functools
import math

import jax
import jax.numpy as jnp
from jax import lax
from jax.experimental import pallas as pl
from jax.experimental.pallas import tpu as pltpu
from jax.sharding import PartitionSpec as P

D = 3072
ROWS = 128
WIDTH = 768
TOK = 1024
N_TOK = 8
N_Y = 4
QUARTER = WIDTH // N_Y
EIGHTH = QUARTER // 2
SHARE = ROWS // 2
PIECES = 4
MAX_COPIES = 200

norm_eps = 1e-06
GRAD_SCALE = 1.0 / math.sqrt(8192)
MESH = pl.DeviceIdType.MESH
BF16 = jnp.bfloat16
F32 = jnp.float32


def gelu_pair(pre_act):
    cdf_part = 0.5 * (1.0 + lax.erf(pre_act * (1.0 / math.sqrt(2.0))))
    dens_part = jnp.exp(-0.5 * pre_act * pre_act) * (1.0 / math.sqrt(2.0 * math.pi))
    return (pre_act * cdf_part, cdf_part + pre_act * dens_part)


def dot(left_op, right_op):
    return jnp.dot(left_op, right_op, preferred_element_type=F32)


def right_contract(left_op, right_op):
    return lax.dot_general(
        left_op, right_op, (((1,), (1,)), ((), ())), preferred_element_type=F32
    )


def row_contract(left_op, right_op):
    return lax.dot_general(
        left_op, right_op, (((0,), (0,)), ((), ())), preferred_element_type=F32
    )


def block(start, size):
    return pl.ds(start if isinstance(start, int) else pl.multiple_of(start, 16), size)


def kernel(
    tok_ref, win_ref, wout_ref, gain_ref, cot_ref,
    mixed_ref, gin_ref, gwin_ref, gwout_ref,
    winc, woutc, xf, cf, pf, rf, pb, rb, slopes, hid, ghid,
    branch, zf, gnorm, zb, stat_out, stat_in, totals, scaled,
    dw, anti, near, qsum, far, ssem, rsem, lsem,
):
    dp, z, h = lax.axis_index("dp"), lax.axis_index("tok"), lax.axis_index("hid")
    y, xh = dp // 2, dp % 2
    xl, c = h // 2, h % 2
    zp, zm = (dp, (z + 1) % N_TOK, h), (dp, (z + N_TOK - 1) % N_TOK, h)
    sib = (dp, z, xl * 2 + 1 - c)
    xn = (dp, z, (1 - xl) * 2 + c)
    diag = (dp, z, (1 - xl) * 2 + 1 - c)
    yp, ym = (((y + 1) % N_Y) * 2 + xh, z, h), (((y + N_Y - 1) % N_Y) * 2 + xh, z, h)
    xo = (y * 2 + 1 - xh, z, h)
    peers = (zp, zm, sib, xn, diag, yp, ym, xo)

    barrier = pltpu.get_barrier_semaphore()
    for peer in peers:
        pl.semaphore_signal(barrier, inc=1, device_id=peer, device_id_type=MESH)
    pl.semaphore_wait(barrier, len(peers))

    sent = []

    def send(src, dst, peer):
        i = len(sent)
        copy = pltpu.make_async_remote_copy(
            src_ref=src, dst_ref=dst, send_sem=ssem.at[i], recv_sem=rsem.at[i],
            device_id=peer, device_id_type=MESH,
        )
        copy.start()
        sent.append(copy)
        return copy

    own_half, sib_half = c * WIDTH, (1 - c) * WIDTH
    lane_own = pl.ds(pl.multiple_of(own_half, WIDTH), WIDTH)
    lane_sib = pl.ds(pl.multiple_of(sib_half, WIDTH), WIDTH)
    local = [
        pltpu.make_async_copy(wout_ref.at[lane_own, :], woutc.at[c], lsem.at[0]),
        pltpu.make_async_copy(win_ref.at[:, lane_own], winc.at[c], lsem.at[1]),
        pltpu.make_async_copy(cot_ref, cf.at[c, block(0, ROWS)], lsem.at[2]),
    ]
    for copy in local:
        copy.start()

    def slot(r, lo=0, size=ROWS):
        return block(r * ROWS + lo, size)

    def ring_first(src, buf):
        return [
            (send(src, buf.at[c, slot(1)], zp),),
            (send(src, buf.at[c, slot(2)], zm),),
            send(src, buf.at[c, slot(0)], sib),
        ]

    ring = {"c": {}, "x": {}}
    sib_copies = {"c": {}, "x": {}}
    bufs = {"c": cf, "x": xf}

    def start_ring(name, src):
        up, down, across = ring_first(src, bufs[name])
        ring[name][1] = up + down
        sib_copies[name][0] = across

    def ring_wait(name, k):
        buf = bufs[name]
        for copy in ring[name][k]:
            copy.wait_recv()
        for r in (2 * k - 1, 2 * k) if k < 4 else (7,):
            sib_copies[name][r] = send(buf.at[c, slot(r)], buf.at[c, slot(r)], sib)

    def ring_forward(name, k):
        buf = bufs[name]
        a, b = 2 * k - 1, 2 * k
        if k < 3:
            ring[name][k + 1] = (
                send(buf.at[c, slot(a)], buf.at[c, slot(a + 2)], zp),
                send(buf.at[c, slot(b)], buf.at[c, slot(b + 2)], zm),
            )
        else:
            lo, hi = (0, SHARE), (SHARE, SHARE)
            ring[name][4] = (
                send(buf.at[c, slot(a, *lo)], buf.at[c, slot(7, *lo)], zp),
                send(buf.at[c, slot(b, *hi)], buf.at[c, slot(7, *hi)], zm),
            )

    start_ring("c", cot_ref)
    weight_copies = [
        send(wout_ref.at[lane_sib, :], woutc.at[c], sib),
        send(win_ref.at[:, lane_sib], winc.at[c], sib),
    ]

    lanes = lax.broadcasted_iota(jnp.int32, (ROWS, ROWS), 1)

    def share_stats(i, first, second):
        stat_out[i] = jnp.where(lanes == 0, first, second).T[0:8]
        return [
            send(stat_out.at[i], stat_in.at[i, j], peer)
            for j, peer in enumerate((xn, diag, sib))
        ]

    def total_stats(i, copies):
        for copy in copies:
            copy.wait_recv()
        total = (stat_out[i] + stat_in[i, 2]) + (stat_in[i, 0] + stat_in[i, 1])
        columns = jnp.concatenate([total] * (ROWS // 8), axis=0).T
        return columns[:, 0:1], columns[:, 1:2]

    tok_float = tok_ref[...].astype(F32)
    stats = share_stats(
        0,
        jnp.sum(tok_float, axis=1, keepdims=True),
        jnp.sum(tok_float * tok_float, axis=1, keepdims=True),
    )

    def partial_product(src, weights, dst, r, transposed):
        rows = slot(r)

        def tile(n, carry):
            cols = pl.ds(pl.multiple_of(n * 256, 256), 256)
            if transposed:
                total = right_contract(src[0, rows], weights[0, cols, :])
                total += right_contract(src[1, rows], weights[1, cols, :])
            else:
                total = dot(src[0, rows], weights[0, :, cols])
                total += dot(src[1, rows], weights[1, :, cols])
            dst[rows, cols] = total.astype(BF16)
            return carry

        lax.fori_loop(0, 3, tile, 0)

    partial_copies = {"f": {}, "b": {}}

    def send_partial(name, part, landing, r):
        partial_copies[name][r] = send(
            part.at[block(r * ROWS + (1 - xl) * SHARE, SHARE)],
            landing.at[block(r * SHARE, SHARE)],
            xn,
        )

    def f1(r):
        sib_copies["x"][r].wait_recv()
        partial_product(xf, winc, pf, r, False)
        send_partial("f", pf, rf, r)

    def b1(r):
        sib_copies["c"][r].wait_recv()
        partial_product(cf, woutc, pb, r, True)
        send_partial("b", pb, rb, r)

    share_copies = {"f": {}, "b": {}}
    whole_copies = {"f": {}, "b": {}}

    def send_share(name, buf, r):
        mine = buf.at[c, block(r * ROWS + xl * SHARE, SHARE)]
        share_copies[name][r] = send(mine, mine, xn)

    def f2(r):
        partial_copies["f"][r].wait_recv()

        def tile(n, carry):
            k = n * 16
            pre_act = pf[block(r * ROWS + xl * SHARE + k, 16), :].astype(F32)
            pre_act += rf[block(r * SHARE + k, 16), :].astype(F32)
            act, slope = gelu_pair(pre_act)
            slopes[block(r * SHARE + k, 16), :] = slope
            hid[c, block(r * ROWS + xl * SHARE + k, 16), :] = act.astype(BF16)
            return carry

        lax.fori_loop(0, SHARE // 16, tile, 0)
        send_share("f", hid, r)

    def b2(r):
        partial_copies["b"][r].wait_recv()

        def tile(n, carry):
            k = n * 16
            grad = pb[block(r * ROWS + xl * SHARE + k, 16), :].astype(F32)
            grad += rb[block(r * SHARE + k, 16), :].astype(F32)
            grad *= slopes[block(r * SHARE + k, 16), :]
            ghid[c, block(r * ROWS + xl * SHARE + k, 16), :] = grad.astype(BF16)
            return carry

        lax.fori_loop(0, SHARE // 16, tile, 0)
        send_share("b", ghid, r)

    def third(name, buf, r):
        share_copies[name][r].wait_recv()
        whole = buf.at[c, slot(r)]
        whole_copies[name][r] = send(whole, whole, sib)

    def f3(r):
        third("f", hid, r)

    def b3(r):
        third("b", ghid, r)

    def whole_wait(name):
        for r in range(N_TOK):
            whole_copies[name][r].wait_recv()

    def product_rows(src, dst, i, transposed):
        rows = block(i * 256, 256)

        def tile(n, carry):
            cols = pl.ds(pl.multiple_of(n * 256, 256), 256)
            if transposed:
                total = right_contract(src[0, rows], win_ref[cols, 0:WIDTH])
                total += right_contract(src[1, rows], win_ref[cols, WIDTH : 2 * WIDTH])
            else:
                total = dot(src[0, rows], wout_ref[0:WIDTH, cols])
                total += dot(src[1, rows], wout_ref[WIDTH : 2 * WIDTH, cols])
            dst[rows, cols] = total.astype(BF16)
            return carry

        lax.fori_loop(0, 3, tile, 0)

    def add_rows(dst, at, src, rows, count):
        def tile(n, carry):
            here = block(at + n * 16, 16)
            there = block(rows + n * 16, 16)
            dst[here, :] = (dst[here, :].astype(F32) + src[there, :].astype(F32)).astype(BF16)
            return carry

        lax.fori_loop(0, count // 16, tile, 0)

    back = {"f": {}, "b": {}}

    def ring_back(name, part, landing, k):
        if k == 4:
            back[name][4] = (
                send(part.at[slot(7, 0, SHARE)], landing.at[slot(5, 0, SHARE)], zm),
                send(part.at[slot(7, SHARE, SHARE)], landing.at[slot(6, SHARE, SHARE)], zp),
            )
            return
        a, b = 2 * k - 1, 2 * k
        for copy in back[name][k + 1]:
            copy.wait_recv()
        if k == 3:
            add_rows(part, a * ROWS, landing, a * ROWS, SHARE)
            add_rows(part, b * ROWS + SHARE, landing, b * ROWS + SHARE, SHARE)
        else:
            add_rows(part, a * ROWS, landing, a * ROWS, ROWS)
            add_rows(part, b * ROWS, landing, b * ROWS, ROWS)
        to_a, to_b = (0, 7) if k == 1 else (a - 2, b - 2)
        back[name][k] = (
            send(part.at[slot(a)], landing.at[slot(to_a)], zm),
            send(part.at[slot(b)], landing.at[slot(to_b)], zp),
        )

    def ring_total(name, part, landing):
        for copy in back[name][1]:
            copy.wait_recv()
        total = part[slot(0), :].astype(F32) + landing[slot(0), :].astype(F32)
        return total + landing[slot(7), :].astype(F32)

    qa, qb, qo = (y + 1) % N_Y, (y + N_Y - 1) % N_Y, (y + 2) % N_Y

    def weight_product(p):
        def tile(n, carry):
            cols = pl.ds(pl.multiple_of(n * 256, 256), 256)
            if p < 2:
                total = row_contract(hid[p, :, cols], cf[c])
            else:
                total = row_contract(xf[c, :, cols], ghid[p - 2])
            dw[p, cols, :] = (total * GRAD_SCALE).astype(BF16)
            return carry

        lax.fori_loop(0, 3, tile, 0)

    first_hop, second_hop, far_copies, spread, spread_on = {}, {}, {}, {}, {}
    low, high = block(0, EIGHTH), block(EIGHTH, EIGHTH)

    def r1(p):
        part = dw.at[p]
        first_hop[p] = (
            send(part.at[block(qo * QUARTER, EIGHTH)], anti.at[p, low], yp),
            send(part.at[block(qo * QUARTER + EIGHTH, EIGHTH)], anti.at[p, high], ym),
        )
        second_hop[p] = (
            send(part.at[block(qa * QUARTER + EIGHTH, EIGHTH)], near.at[p, 0, high], yp),
            send(part.at[block(qb * QUARTER, EIGHTH)], near.at[p, 1, low], ym),
        )

    def r2(p):
        part = dw.at[p]
        for copy in first_hop[p]:
            copy.wait_recv()
        add_rows(part, qa * QUARTER, anti.at[p], 0, EIGHTH)
        add_rows(part, qb * QUARTER + EIGHTH, anti.at[p], EIGHTH, EIGHTH)
        second_hop[p] += (
            send(part.at[block(qa * QUARTER, EIGHTH)], near.at[p, 0, low], yp),
            send(part.at[block(qb * QUARTER + EIGHTH, EIGHTH)], near.at[p, 1, high], ym),
        )

    def r3(p):
        for copy in second_hop[p]:
            copy.wait_recv()

        def tile(n, carry):
            rows = block(n * 16, 16)
            total = dw[p, block(y * QUARTER + n * 16, 16), :].astype(F32)
            total += near[p, 0, rows, :].astype(F32) + near[p, 1, rows, :].astype(F32)
            qsum[p, rows, :] = total.astype(BF16)
            return carry

        lax.fori_loop(0, QUARTER // 16, tile, 0)
        far_copies[p] = send(qsum.at[p], far.at[p], xo)

    def out_rows(p, start, size):
        if p < 2:
            return gwout_ref, (block(p * WIDTH + start, size), slice(None))
        return gwin_ref, (block(start, size), pl.ds((p - 2) * WIDTH, WIDTH))

    def out_at(p, start, size):
        ref, where = out_rows(p, start, size)
        return ref.at[where]

    def r4(p):
        far_copies[p].wait_recv()

        def tile(n, carry):
            rows = block(n * 16, 16)
            total = qsum[p, rows, :].astype(F32) + far[p, rows, :].astype(F32)
            ref, where = out_rows(p, y * QUARTER + n * 16, 16)
            ref[where] = total.astype(BF16)
            return carry

        lax.fori_loop(0, QUARTER // 16, tile, 0)
        own = out_at(p, y * QUARTER, QUARTER)
        spread[p] = (send(own, own, yp), send(own, own, ym))

    def r5(p):
        for copy in spread[p]:
            copy.wait_recv()
        behind = out_at(p, qb * QUARTER, EIGHTH)
        ahead = out_at(p, qa * QUARTER + EIGHTH, EIGHTH)
        spread_on[p] = (send(behind, behind, yp), send(ahead, ahead, ym))

    def r6(p):
        for copy in spread_on[p]:
            copy.wait_recv()

    local[0].wait()
    local[2].wait()
    weight_copies[0].wait_recv()
    b1(0)
    row_sum, square_sum = total_stats(0, stats)
    row_mean = row_sum / D
    row_rstd = lax.rsqrt(square_sum / D - row_mean * row_mean + norm_eps)
    totals[...] = jnp.where(lanes == 0, row_mean, row_rstd)
    centred = (tok_float - row_mean) * row_rstd
    xf[c, slot(0)] = (centred * gain_ref[...]).astype(BF16)
    start_ring("x", xf.at[c, slot(0)])
    local[1].wait()
    weight_copies[1].wait_recv()
    f1(0)
    ring_wait("c", 1)
    b1(1), b1(2)
    ring_wait("x", 1), ring_forward("x", 1)
    f1(1), f1(2), f2(0)
    ring_wait("x", 2), ring_forward("x", 2), ring_forward("c", 1)
    f1(3), f1(4), f2(1), f2(2), f3(0)
    ring_wait("x", 3), ring_forward("x", 3)
    f1(5), f1(6), f2(3), f2(4), f3(1), f3(2)
    ring_wait("c", 2), ring_forward("c", 2)
    ring_wait("x", 4)
    f1(7), f2(5), f2(6), f3(3), f3(4)
    b1(3), b1(4)
    f2(7)
    ring_wait("c", 3), ring_forward("c", 3)
    f3(5), f3(6)
    b1(5), b1(6)
    f3(7)
    b2(0), b2(1), b2(2)
    ring_wait("c", 4)
    b1(7)
    whole_wait("f")
    weight_product(0), r1(0)
    weight_product(1), r1(1)
    b2(3), b2(4), b3(0), b3(1), b3(2)
    product_rows(hid, branch, 3, False), ring_back("f", branch, zf, 4)
    r2(0), r2(1)
    b2(5), b2(6), b3(3), b3(4)
    product_rows(hid, branch, 2, False), ring_back("f", branch, zf, 3)
    r3(0), b2(7), b3(5), b3(6)
    product_rows(hid, branch, 1, False), ring_back("f", branch, zf, 2)
    r3(1), r4(0), b3(7)
    product_rows(hid, branch, 0, False), ring_back("f", branch, zf, 1)
    r4(1)
    whole_wait("b")
    weight_product(2), r1(2)
    weight_product(3), r1(3)
    product_rows(ghid, gnorm, 3, True), ring_back("b", gnorm, zb, 4)
    r5(0), r2(2)
    r5(1), r2(3)
    product_rows(ghid, gnorm, 2, True), ring_back("b", gnorm, zb, 3)
    mixed_ref[...] = (
        tok_ref[...].astype(F32) + ring_total("f", branch, zf)
    ).astype(BF16)
    product_rows(ghid, gnorm, 1, True), ring_back("b", gnorm, zb, 2)
    r3(2)
    product_rows(ghid, gnorm, 0, True), ring_back("b", gnorm, zb, 1)
    r3(3), r4(2)

    grad_scaled = ring_total("b", gnorm, zb) * gain_ref[...]
    scaled[...] = grad_scaled
    row_mean, row_rstd = totals[:, 0:1], totals[:, 1:2]
    centred = (tok_ref[...].astype(F32) - row_mean) * row_rstd
    stats = share_stats(
        1,
        jnp.sum(grad_scaled, axis=1, keepdims=True),
        jnp.sum(grad_scaled * centred, axis=1, keepdims=True),
    )
    r4(3)
    r5(2)
    first_sum, second_sum = total_stats(1, stats)
    gin_ref[...] = (
        cot_ref[...].astype(F32)
        + row_rstd * (scaled[...] - first_sum / D - centred * (second_sum / D))
    ).astype(BF16)
    r5(3)
    for p in range(PIECES):
        r6(p)
    for copy in sent:
        copy.wait_send()


def shards(tokens, w_in, w_out, gain, cotangent):
    vmem = pl.BlockSpec(memory_space=pltpu.VMEM)
    return pl.pallas_call(
        kernel,
        out_shape=(
            jax.ShapeDtypeStruct((ROWS, WIDTH), BF16),
            jax.ShapeDtypeStruct((ROWS, WIDTH), BF16),
            jax.ShapeDtypeStruct((WIDTH, 2 * WIDTH), BF16),
            jax.ShapeDtypeStruct((2 * WIDTH, WIDTH), BF16),
        ),
        in_specs=[vmem] * 5,
        out_specs=(vmem,) * 4,
        scratch_shapes=[
            pltpu.VMEM((2, WIDTH, WIDTH), BF16),
            pltpu.VMEM((2, WIDTH, WIDTH), BF16),
            pltpu.VMEM((2, TOK, WIDTH), BF16),
            pltpu.VMEM((2, TOK, WIDTH), BF16),
            pltpu.VMEM((TOK, WIDTH), BF16),
            pltpu.VMEM((TOK // 2, WIDTH), BF16),
            pltpu.VMEM((TOK, WIDTH), BF16),
            pltpu.VMEM((TOK // 2, WIDTH), BF16),
            pltpu.VMEM((TOK // 2, WIDTH), F32),
            pltpu.VMEM((2, TOK, WIDTH), BF16),
            pltpu.VMEM((2, TOK, WIDTH), BF16),
            pltpu.VMEM((TOK, WIDTH), BF16),
            pltpu.VMEM((TOK, WIDTH), BF16),
            pltpu.VMEM((TOK, WIDTH), BF16),
            pltpu.VMEM((TOK, WIDTH), BF16),
            pltpu.VMEM((2, 8, ROWS), F32),
            pltpu.VMEM((2, 3, 8, ROWS), F32),
            pltpu.VMEM((ROWS, ROWS), F32),
            pltpu.VMEM((ROWS, WIDTH), F32),
            pltpu.VMEM((PIECES, WIDTH, WIDTH), BF16),
            pltpu.VMEM((PIECES, QUARTER, WIDTH), BF16),
            pltpu.VMEM((PIECES, 2, QUARTER, WIDTH), BF16),
            pltpu.VMEM((PIECES, QUARTER, WIDTH), BF16),
            pltpu.VMEM((PIECES, QUARTER, WIDTH), BF16),
            pltpu.SemaphoreType.DMA((MAX_COPIES,)),
            pltpu.SemaphoreType.DMA((MAX_COPIES,)),
            pltpu.SemaphoreType.DMA((3,)),
        ],
        compiler_params=pltpu.CompilerParams(
            collective_id=0, has_side_effects=True, vmem_limit_bytes=60 << 20
        ),
        cost_estimate=pl.CostEstimate(
            flops=6 * 2 * TOK * WIDTH * 2 * WIDTH, bytes_accessed=12 << 20, transcendentals=0
        ),
        name="mlp_block",
    )(tokens, w_in, w_out, gain.reshape(1, WIDTH), cotangent)


def solution(mesh):
    in_specs = (
        P(("dp", "tok"), "hid"),
        P("hid", "tok"),
        P("tok", "hid"),
        P("hid"),
        P(("dp", "tok"), "hid"),
    )
    out_specs = (P(("dp", "tok"), "hid"), P(("dp", "tok"), "hid"), P("hid", "tok"), P("tok", "hid"))
    return jax.shard_map(shards, mesh=mesh, in_specs=in_specs, out_specs=out_specs, check_vma=False)
```

time: 663 us -> 175 us (0.26)
  waiting for transfers between devices: 579 us -> 0 us
  Pallas kernels: 0 us -> 163 us
  matrix products: 36.8 us -> 0 us
  blocking collectives: 18 us -> 0 us
  between operations: 14.2 us -> 0.64 us
  other arithmetic: 9.42 us -> 0 us
    reduce_scatter x6 -> x0, waiting for transfers between devices: 302 us -> none  [the longest x1 84.7 us: shards(): lax.psum_scatter(in_local.astype(jnp.bfloat16), 'dp', scatter_dimension=0...]
    all_gather x6 -> x0, waiting for transfers between devices: 276 us -> none  [the longest x1 63.9 us: shards(): lax.all_gather(out_summed.astype(jnp.bfloat16), 'dp', axis=0, tiled=True)]
    pallas_call x0 -> x1, Pallas kernels: none -> 163 us  [shards(): pl.pallas_call(kernel, out_shape=(jax.ShapeDtypeStruct((ROWS, WIDTH), BF1...]
    dot_general x6 -> x0, matrix products: 36.8 us -> none  [the longest x2 12.8 us: row_contract(): lax.dot_general(left_op, right_op, (((0,), (0,)), ((), ())), preferred_el...]
    psum x2 -> x0, blocking collectives: 18 us -> none  [the longest x1 9.7 us: shards(): lax.psum((jnp.sum(grad_scaled, axis=1), jnp.sum(grad_scaled * centred, ax...]
    convert_element_type x3 -> x0, other arithmetic: 7.05 us -> none  [the longest x1 3.33 us: shards(): grad_share = (grad_act * slopes).astype(jnp.bfloat16)]
  transfers between devices with their start and end apart: 12 -> 0, of which waited for: 12 -> 0; matrix products, arithmetic and copies ran while one was open for 6% -> 0% of each run, Pallas kernels for 0% -> 0%
where the time goes in v1:
time: 175 us; the launch traced here: 173 us
  Pallas kernels  163 us (93%)
  local copies, waits for them, and re-layouts  9.28 us (5%)
    pallas_call x1, Pallas kernels, shards(): pl.pallas_call(kernel, out_shape=(jax.ShapeDtypeStruct((ROWS, WIDTH), BF1...  163 us
    unnamed x6, local copies, waits for them, and re-layouts  8.01 us

profile of v1, /device:TPU:1, one launch (start us, length us, event | category | flops | bytes accessed | tf_op | source)
XLA Modules:
  0.0 172.8 jit_solution(663368279870476476)
XLA Ops:
  0.6 1.3 reshape.11.gain_ref
  1.9 162.9 %mlp_block.1 = (bf16[128,768]{1,0:T(8,128)(2,1)}, bf16[128,768]{1,0:T(8,128)(2,1)}, bf16[768,1536]{1,0:T(8,128)(2,1)}, bf16[1536,768]{1,0:T(8,128)(2,1)}) custom-call(bf16[128,768]{1,0:T(8,128)(2,1)} %tok_ref.1, bf16[768,1536]{1,0:T(8,128)(2,1)} %win_ref.1, bf16[1536,768]{1,0:T(8,128)(2,1)} %wout_ref.1, f32[1,768]{1,0:T(1,128)} %reshape.11.gain_ref, ...), custom_call_target="tpu_custom_call" | custom-call | flops 14495514624 | bytes 12582912 | tf_op jit(solution)/shard_map/mlp_block/pallas_call | solution.py:487
  164.8 1.6 copy.13
  166.4 1.6 copy.14
  168.0 0.0 copy-start
  168.0 3.4 %copy.15 = bf16[768,1536]{1,0:T(8,128)(2,1)} copy(bf16[768,1536]{1,0:T(8,128)(2,1)} %get-tuple-element.10) | data formatting | bytes 4718592
  171.4 0.0 copy-done
  171.4 1.4 copy.16
Async XLA Ops:
  168.0 3.4 %copy-start = (bf16[1536,768]{1,0:T(8,128)(2,1)S(1)}, bf16[1536,768]{1,0:T(8,128)(2,1)}, u32[]{:S(2)}) copy-start(bf16[1536,768]{1,0:T(8,128)(2,1)} %get-tuple-element.11) | copy-start | bytes 7077892

commit v2 on v1

--- a/solution.py
+++ b/solution.py
@@ -18,6 +18,7 @@
 EIGHTH = QUARTER // 2
 SHARE = ROWS // 2
 PIECES = 4
+X_LAST = (1, 2)
 MAX_COPIES = 200
 
 norm_eps = 1e-06
@@ -58,7 +59,7 @@
     mixed_ref, gin_ref, gwin_ref, gwout_ref,
     winc, woutc, xf, cf, pf, rf, pb, rb, slopes, hid, ghid,
     branch, zf, gnorm, zb, stat_out, stat_in, totals, scaled,
-    dw, anti, near, qsum, far, ssem, rsem, lsem,
+    dw, anti, near, qsum, far, tok_buf, win_buf, wout_buf, ssem, rsem, lsem,
 ):
     dp, z, h = lax.axis_index("dp"), lax.axis_index("tok"), lax.axis_index("hid")
     y, xh = dp // 2, dp % 2
@@ -71,10 +72,24 @@
     xo = (y * 2 + 1 - xh, z, h)
     peers = (zp, zm, sib, xn, diag, yp, ym, xo)
 
+    own_half, sib_half = c * WIDTH, (1 - c) * WIDTH
+    lane_own = pl.ds(pl.multiple_of(own_half, WIDTH), WIDTH)
+    lane_sib = pl.ds(pl.multiple_of(sib_half, WIDTH), WIDTH)
+
     barrier = pltpu.get_barrier_semaphore()
     for peer in peers:
         pl.semaphore_signal(barrier, inc=1, device_id=peer, device_id_type=MESH)
-    pl.semaphore_wait(barrier, len(peers))
+
+    local = [
+        pltpu.make_async_copy(tok_ref, tok_buf, lsem.at[0]),
+        pltpu.make_async_copy(cot_ref, cf.at[c, pl.ds(0, ROWS)], lsem.at[1]),
+        pltpu.make_async_copy(wout_ref.at[lane_own, :], woutc.at[c], lsem.at[2]),
+        pltpu.make_async_copy(win_ref.at[:, lane_own], winc.at[c], lsem.at[3]),
+        pltpu.make_async_copy(wout_ref, wout_buf, lsem.at[4]),
+        pltpu.make_async_copy(win_ref, win_buf, lsem.at[5]),
+    ]
+    for copy in local:
+        copy.start()
 
     sent = []
 
@@ -87,17 +102,6 @@
         copy.start()
         sent.append(copy)
         return copy
-
-    own_half, sib_half = c * WIDTH, (1 - c) * WIDTH
-    lane_own = pl.ds(pl.multiple_of(own_half, WIDTH), WIDTH)
-    lane_sib = pl.ds(pl.multiple_of(sib_half, WIDTH), WIDTH)
-    local = [
-        pltpu.make_async_copy(wout_ref.at[lane_own, :], woutc.at[c], lsem.at[0]),
-        pltpu.make_async_copy(win_ref.at[:, lane_own], winc.at[c], lsem.at[1]),
-        pltpu.make_async_copy(cot_ref, cf.at[c, block(0, ROWS)], lsem.at[2]),
-    ]
-    for copy in local:
-        copy.start()
 
     def slot(r, lo=0, size=ROWS):
         return block(r * ROWS + lo, size)
@@ -140,12 +144,6 @@
                 send(buf.at[c, slot(b, *hi)], buf.at[c, slot(7, *hi)], zm),
             )
 
-    start_ring("c", cot_ref)
-    weight_copies = [
-        send(wout_ref.at[lane_sib, :], woutc.at[c], sib),
-        send(win_ref.at[:, lane_sib], winc.at[c], sib),
-    ]
-
     lanes = lax.broadcasted_iota(jnp.int32, (ROWS, ROWS), 1)
 
     def share_stats(i, first, second):
@@ -162,28 +160,27 @@
         columns = jnp.concatenate([total] * (ROWS // 8), axis=0).T
         return columns[:, 0:1], columns[:, 1:2]
 
-    tok_float = tok_ref[...].astype(F32)
-    stats = share_stats(
-        0,
-        jnp.sum(tok_float, axis=1, keepdims=True),
-        jnp.sum(tok_float * tok_float, axis=1, keepdims=True),
-    )
+    local[0].wait()
+    tok_float = tok_buf[...].astype(F32)
+    tok_sum = jnp.sum(tok_float, axis=1, keepdims=True)
+    tok_squares = jnp.sum(tok_float * tok_float, axis=1, keepdims=True)
+    pl.semaphore_wait(barrier, len(peers))
+    stats = share_stats(0, tok_sum, tok_squares)
+    local[1].wait()
+    start_ring("c", cf.at[c, slot(0)])
+    weight_copies = [
+        send(wout_ref.at[lane_sib, :], woutc.at[c], sib),
+        send(win_ref.at[:, lane_sib], winc.at[c], sib),
+    ]
 
     def partial_product(src, weights, dst, r, transposed):
         rows = slot(r)
-
-        def tile(n, carry):
-            cols = pl.ds(pl.multiple_of(n * 256, 256), 256)
-            if transposed:
-                total = right_contract(src[0, rows], weights[0, cols, :])
-                total += right_contract(src[1, rows], weights[1, cols, :])
-            else:
-                total = dot(src[0, rows], weights[0, :, cols])
-                total += dot(src[1, rows], weights[1, :, cols])
-            dst[rows, cols] = total.astype(BF16)
-            return carry
-
-        lax.fori_loop(0, 3, tile, 0)
+        if transposed:
+            total = right_contract(src[0, rows], weights[0])
+            total += right_contract(src[1, rows], weights[1])
+        else:
+            total = dot(src[0, rows], weights[0]) + dot(src[1, rows], weights[1])
+        dst[rows, :] = total.astype(BF16)
 
     partial_copies = {"f": {}, "b": {}}
 
@@ -195,11 +192,17 @@
         )
 
     def f1(r):
+        if r == 0:
+            local[3].wait()
+            weight_copies[1].wait_recv()
         sib_copies["x"][r].wait_recv()
         partial_product(xf, winc, pf, r, False)
         send_partial("f", pf, rf, r)
 
     def b1(r):
+        if r == 0:
+            local[2].wait()
+            weight_copies[0].wait_recv()
         sib_copies["c"][r].wait_recv()
         partial_product(cf, woutc, pb, r, True)
         send_partial("b", pb, rb, r)
@@ -251,25 +254,28 @@
     def b3(r):
         third("b", ghid, r)
 
+    waited = {"f": False, "b": False}
+
     def whole_wait(name):
+        waited[name] = True
         for r in range(N_TOK):
             whole_copies[name][r].wait_recv()
 
     def product_rows(src, dst, i, transposed):
+        if not waited["b" if transposed else "f"]:
+            whole_wait("b" if transposed else "f")
         rows = block(i * 256, 256)
-
-        def tile(n, carry):
-            cols = pl.ds(pl.multiple_of(n * 256, 256), 256)
-            if transposed:
-                total = right_contract(src[0, rows], win_ref[cols, 0:WIDTH])
-                total += right_contract(src[1, rows], win_ref[cols, WIDTH : 2 * WIDTH])
-            else:
-                total = dot(src[0, rows], wout_ref[0:WIDTH, cols])
-                total += dot(src[1, rows], wout_ref[WIDTH : 2 * WIDTH, cols])
-            dst[rows, cols] = total.astype(BF16)
-            return carry
-
-        lax.fori_loop(0, 3, tile, 0)
+        if transposed:
+            if i == 3:
+                local[5].wait()
+            total = right_contract(src[0, rows], win_buf[:, 0:WIDTH])
+            total += right_contract(src[1, rows], win_buf[:, WIDTH : 2 * WIDTH])
+        else:
+            if i == 3:
+                local[4].wait()
+            total = dot(src[0, rows], wout_buf[0:WIDTH, :])
+            total += dot(src[1, rows], wout_buf[WIDTH : 2 * WIDTH, :])
+        dst[rows, :] = total.astype(BF16)
 
     def add_rows(dst, at, src, rows, count):
         def tile(n, carry):
@@ -313,18 +319,13 @@
     qa, qb, qo = (y + 1) % N_Y, (y + N_Y - 1) % N_Y, (y + 2) % N_Y
 
     def weight_product(p):
-        def tile(n, carry):
-            cols = pl.ds(pl.multiple_of(n * 256, 256), 256)
-            if p < 2:
-                total = row_contract(hid[p, :, cols], cf[c])
-            else:
-                total = row_contract(xf[c, :, cols], ghid[p - 2])
-            dw[p, cols, :] = (total * GRAD_SCALE).astype(BF16)
-            return carry
-
-        lax.fori_loop(0, 3, tile, 0)
-
-    first_hop, second_hop, far_copies, spread, spread_on = {}, {}, {}, {}, {}
+        if p < 2:
+            total = row_contract(hid[p], cf[c])
+        else:
+            total = row_contract(xf[c], ghid[p - 2])
+        dw[p] = (total * GRAD_SCALE).astype(BF16)
+
+    first_hop, second_hop, far_copies, spread, spread_on, across = {}, {}, {}, {}, {}, {}
     low, high = block(0, EIGHTH), block(EIGHTH, EIGHTH)
 
     def r1(p):
@@ -361,7 +362,11 @@
             return carry
 
         lax.fori_loop(0, QUARTER // 16, tile, 0)
-        far_copies[p] = send(qsum.at[p], far.at[p], xo)
+        if p in X_LAST:
+            theirs = block((1 - xh) * EIGHTH, EIGHTH)
+            far_copies[p] = send(qsum.at[p, theirs], far.at[p, low], xo)
+        else:
+            far_copies[p] = send(qsum.at[p], far.at[p], xo)
 
     def out_rows(p, start, size):
         if p < 2:
@@ -374,125 +379,136 @@
 
     def r4(p):
         far_copies[p].wait_recv()
+        mine, count = (xh * EIGHTH, EIGHTH) if p in X_LAST else (0, QUARTER)
 
         def tile(n, carry):
-            rows = block(n * 16, 16)
-            total = qsum[p, rows, :].astype(F32) + far[p, rows, :].astype(F32)
-            ref, where = out_rows(p, y * QUARTER + n * 16, 16)
+            total = qsum[p, block(mine + n * 16, 16), :].astype(F32)
+            total += far[p, block(n * 16, 16), :].astype(F32)
+            ref, where = out_rows(p, y * QUARTER + mine + n * 16, 16)
             ref[where] = total.astype(BF16)
             return carry
 
-        lax.fori_loop(0, QUARTER // 16, tile, 0)
-        own = out_at(p, y * QUARTER, QUARTER)
+        lax.fori_loop(0, count // 16, tile, 0)
+        own = out_at(p, y * QUARTER + mine, count)
         spread[p] = (send(own, own, yp), send(own, own, ym))
+        if p in X_LAST:
+            across[p] = (send(own, own, xo),)
 
     def r5(p):
         for copy in spread[p]:
             copy.wait_recv()
-        behind = out_at(p, qb * QUARTER, EIGHTH)
-        ahead = out_at(p, qa * QUARTER + EIGHTH, EIGHTH)
+        mine, half = (xh * EIGHTH, EIGHTH // 2) if p in X_LAST else (0, EIGHTH)
+        behind = out_at(p, qb * QUARTER + mine, half)
+        ahead = out_at(p, qa * QUARTER + mine + half, half)
         spread_on[p] = (send(behind, behind, yp), send(ahead, ahead, ym))
+        if p in X_LAST:
+            for q in (qb, qa):
+                whole = out_at(p, q * QUARTER + mine, EIGHTH)
+                across[p] += (send(whole, whole, xo),)
 
     def r6(p):
         for copy in spread_on[p]:
             copy.wait_recv()
-
-    local[0].wait()
-    local[2].wait()
-    weight_copies[0].wait_recv()
-    b1(0)
-    row_sum, square_sum = total_stats(0, stats)
-    row_mean = row_sum / D
-    row_rstd = lax.rsqrt(square_sum / D - row_mean * row_mean + norm_eps)
-    totals[...] = jnp.where(lanes == 0, row_mean, row_rstd)
-    centred = (tok_float - row_mean) * row_rstd
-    xf[c, slot(0)] = (centred * gain_ref[...]).astype(BF16)
-    start_ring("x", xf.at[c, slot(0)])
-    local[1].wait()
-    weight_copies[1].wait_recv()
-    f1(0)
-    ring_wait("c", 1)
-    b1(1), b1(2)
-    ring_wait("x", 1), ring_forward("x", 1)
-    f1(1), f1(2), f2(0)
-    ring_wait("x", 2), ring_forward("x", 2), ring_forward("c", 1)
-    f1(3), f1(4), f2(1), f2(2), f3(0)
-    ring_wait("x", 3), ring_forward("x", 3)
-    f1(5), f1(6), f2(3), f2(4), f3(1), f3(2)
-    ring_wait("c", 2), ring_forward("c", 2)
-    ring_wait("x", 4)
-    f1(7), f2(5), f2(6), f3(3), f3(4)
-    b1(3), b1(4)
-    f2(7)
-    ring_wait("c", 3), ring_forward("c", 3)
-    f3(5), f3(6)
-    b1(5), b1(6)
-    f3(7)
-    b2(0), b2(1), b2(2)
-    ring_wait("c", 4)
-    b1(7)
-    whole_wait("f")
-    weight_product(0), r1(0)
-    weight_product(1), r1(1)
-    b2(3), b2(4), b3(0), b3(1), b3(2)
-    product_rows(hid, branch, 3, False), ring_back("f", branch, zf, 4)
-    r2(0), r2(1)
-    b2(5), b2(6), b3(3), b3(4)
-    product_rows(hid, branch, 2, False), ring_back("f", branch, zf, 3)
-    r3(0), b2(7), b3(5), b3(6)
-    product_rows(hid, branch, 1, False), ring_back("f", branch, zf, 2)
-    r3(1), r4(0), b3(7)
-    product_rows(hid, branch, 0, False), ring_back("f", branch, zf, 1)
-    r4(1)
-    whole_wait("b")
-    weight_product(2), r1(2)
-    weight_product(3), r1(3)
-    product_rows(ghid, gnorm, 3, True), ring_back("b", gnorm, zb, 4)
-    r5(0), r2(2)
-    r5(1), r2(3)
-    product_rows(ghid, gnorm, 2, True), ring_back("b", gnorm, zb, 3)
-    mixed_ref[...] = (
-        tok_ref[...].astype(F32) + ring_total("f", branch, zf)
-    ).astype(BF16)
-    product_rows(ghid, gnorm, 1, True), ring_back("b", gnorm, zb, 2)
-    r3(2)
-    product_rows(ghid, gnorm, 0, True), ring_back("b", gnorm, zb, 1)
-    r3(3), r4(2)
-
-    grad_scaled = ring_total("b", gnorm, zb) * gain_ref[...]
-    scaled[...] = grad_scaled
-    row_mean, row_rstd = totals[:, 0:1], totals[:, 1:2]
-    centred = (tok_ref[...].astype(F32) - row_mean) * row_rstd
-    stats = share_stats(
-        1,
-        jnp.sum(grad_scaled, axis=1, keepdims=True),
-        jnp.sum(grad_scaled * centred, axis=1, keepdims=True),
+        if p in X_LAST:
+            whole = out_at(p, qo * QUARTER + xh * EIGHTH, EIGHTH)
+            across[p] += (send(whole, whole, xo),)
+
+    def r7(p):
+        for copy in across[p]:
+            copy.wait_recv()
+
+    state = {}
+
+    def normalize():
+        row_sum, square_sum = total_stats(0, stats)
+        row_mean = row_sum / D
+        row_rstd = lax.rsqrt(square_sum / D - row_mean * row_mean + norm_eps)
+        totals[...] = jnp.where(lanes == 0, row_mean, row_rstd)
+        centred = (tok_float - row_mean) * row_rstd
+        xf[c, slot(0)] = (centred * gain_ref[...]).astype(BF16)
+        start_ring("x", xf.at[c, slot(0)])
+
+    def blk(name, i):
+        if name == "f":
+            product_rows(hid, branch, i, False)
+        else:
+            product_rows(ghid, gnorm, i, True)
+
+    def back_step(name, k):
+        if name == "f":
+            ring_back(name, branch, zf, k)
+        else:
+            ring_back(name, gnorm, zb, k)
+
+    def finish_out():
+        mixed_ref[...] = (
+            tok_buf[...].astype(F32) + ring_total("f", branch, zf)
+        ).astype(BF16)
+
+    def centred_rows():
+        row_mean, row_rstd = totals[:, 0:1], totals[:, 1:2]
+        return (tok_buf[...].astype(F32) - row_mean) * row_rstd, row_rstd
+
+    def share_grad():
+        grad_scaled = ring_total("b", gnorm, zb) * gain_ref[...]
+        scaled[...] = grad_scaled
+        centred, _ = centred_rows()
+        state["grad"] = share_stats(
+            1,
+            jnp.sum(grad_scaled, axis=1, keepdims=True),
+            jnp.sum(grad_scaled * centred, axis=1, keepdims=True),
+        )
+
+    def finish_grad():
+        first_sum, second_sum = total_stats(1, state["grad"])
+        centred, row_rstd = centred_rows()
+        gin_ref[...] = (
+            cf[c, slot(0)].astype(F32)
+            + row_rstd * (scaled[...] - first_sum / D - centred * (second_sum / D))
+        ).astype(BF16)
+
+    def product(p):
+        if p in (0, 1) and not waited["f"]:
+            whole_wait("f")
+        if p in (2, 3) and not waited["b"]:
+            whole_wait("b")
+        weight_product(p)
+        r1(p)
+
+    schedule = (
+        (b1, 0), (normalize,), (ring_wait, "c", 1), (f1, 0), (b1, 2), (f2, 0), (ring_wait, "x", 1), (f1, 2),
+        (ring_forward, "x", 1), (f1, 1), (f2, 2), (ring_wait, "x", 2), (ring_forward, "x", 2), (f2, 1),
+        (f1, 3), (ring_forward, "c", 1), (f1, 4), (ring_wait, "x", 3), (f2, 3), (f3, 1), (f1, 6), (f1, 5),
+        (f2, 4), (ring_wait, "c", 2), (ring_forward, "x", 3), (f3, 2), (ring_wait, "x", 4), (f3, 3),
+        (ring_forward, "c", 2), (f1, 7), (f2, 5), (f2, 7), (ring_wait, "c", 3), (f2, 6), (f3, 0), (b1, 3),
+        (f3, 7), (ring_forward, "c", 3), (f3, 4), (b2, 2), (f3, 5), (b2, 0), (f3, 6), (b1, 1), (blk, "f", 3),
+        (ring_wait, "c", 4), (b1, 6), (b1, 5), (b1, 4), (b2, 3), (product, 1), (b2, 1), (b3, 2), (r2, 1),
+        (b2, 6), (b1, 7), (blk, "f", 2), (product, 0), (r3, 1), (b2, 7), (b3, 3), (back_step, "f", 4),
+        (b3, 1), (b3, 6), (b2, 5), (b2, 4), (r2, 0), (b3, 0), (r4, 1), (b3, 5), (blk, "f", 1), (b3, 7),
+        (r3, 0), (r5, 1), (b3, 4), (product, 2), (r2, 2), (back_step, "f", 3), (blk, "f", 0), (blk, "b", 3),
+        (product, 3), (back_step, "f", 2), (blk, "b", 1), (r3, 2), (blk, "b", 2), (blk, "b", 0), (r2, 3),
+        (back_step, "b", 4), (r4, 2), (back_step, "b", 3), (r4, 0), (r3, 3), (back_step, "b", 2), (r5, 2),
+        (r4, 3), (r6, 1), (back_step, "b", 1), (r5, 0), (back_step, "f", 1), (r6, 2), (share_grad,), (r5, 3),
+        (finish_grad,), (finish_out,), (r6, 0), (r7, 2), (r7, 1), (r6, 3),
     )
-    r4(3)
-    r5(2)
-    first_sum, second_sum = total_stats(1, stats)
-    gin_ref[...] = (
-        cot_ref[...].astype(F32)
-        + row_rstd * (scaled[...] - first_sum / D - centred * (second_sum / D))
-    ).astype(BF16)
-    r5(3)
-    for p in range(PIECES):
-        r6(p)
+    for step, *where in schedule:
+        step(*where)
     for copy in sent:
         copy.wait_send()
 
 
 def shards(tokens, w_in, w_out, gain, cotangent):
     vmem = pl.BlockSpec(memory_space=pltpu.VMEM)
+    anywhere = pl.BlockSpec(memory_space=pl.ANY)
     return pl.pallas_call(
         kernel,
         out_shape=(
-            jax.ShapeDtypeStruct((ROWS, WIDTH), BF16),
-            jax.ShapeDtypeStruct((ROWS, WIDTH), BF16),
-            jax.ShapeDtypeStruct((WIDTH, 2 * WIDTH), BF16),
-            jax.ShapeDtypeStruct((2 * WIDTH, WIDTH), BF16),
+            pltpu.VMEM((ROWS, WIDTH), BF16),
+            pltpu.VMEM((ROWS, WIDTH), BF16),
+            pltpu.VMEM((WIDTH, 2 * WIDTH), BF16),
+            pltpu.VMEM((2 * WIDTH, WIDTH), BF16),
         ),
-        in_specs=[vmem] * 5,
+        in_specs=[anywhere, anywhere, anywhere, vmem, anywhere],
         out_specs=(vmem,) * 4,
         scratch_shapes=[
             pltpu.VMEM((2, WIDTH, WIDTH), BF16),
@@ -519,12 +535,15 @@
             pltpu.VMEM((PIECES, 2, QUARTER, WIDTH), BF16),
             pltpu.VMEM((PIECES, QUARTER, WIDTH), BF16),
             pltpu.VMEM((PIECES, QUARTER, WIDTH), BF16),
+            pltpu.VMEM((ROWS, WIDTH), BF16),
+            pltpu.VMEM((WIDTH, 2 * WIDTH), BF16),
+            pltpu.VMEM((2 * WIDTH, WIDTH), BF16),
             pltpu.SemaphoreType.DMA((MAX_COPIES,)),
             pltpu.SemaphoreType.DMA((MAX_COPIES,)),
-            pltpu.SemaphoreType.DMA((3,)),
+            pltpu.SemaphoreType.DMA((6,)),
         ],
         compiler_params=pltpu.CompilerParams(
-            collective_id=0, has_side_effects=True, vmem_limit_bytes=60 << 20
+            collective_id=0, has_side_effects=True, vmem_limit_bytes=54 << 20
         ),
         cost_estimate=pl.CostEstimate(
             flops=6 * 2 * TOK * WIDTH * 2 * WIDTH, bytes_accessed=12 << 20, transcendentals=0

time: 175 us -> 148 us (0.85)
  Pallas kernels: 163 us -> 141 us
  local copies, waits for them, and re-layouts: 9.28 us -> 5.43 us
    pallas_call x1, Pallas kernels: 163 us -> 141 us  [shards(): pl.pallas_call(kernel, out_shape=(pltpu.VMEM((ROWS, WIDTH), BF16), pltpu....]
    unnamed x6 -> x4, local copies, waits for them, and re-layouts: 8.01 us -> 4.17 us
where the time goes in v2:
time: 148 us; the launch traced here: 147 us
  Pallas kernels  141 us (95%)
  local copies, waits for them, and re-layouts  5.43 us (4%)
    pallas_call x1, Pallas kernels, shards(): pl.pallas_call(kernel, out_shape=(pltpu.VMEM((ROWS, WIDTH), BF16), pltpu....  141 us
    unnamed x4, local copies, waits for them, and re-layouts  4.17 us

profile of v2, /device:TPU:1, one launch (start us, length us, event | category | flops | bytes accessed | tf_op | source)
XLA Modules:
  0.0 147.0 jit_solution(4802888097484999831)
XLA Ops:
  0.6 1.3 reshape.11.gain_ref
  1.9 140.9 %mlp_block.1 = (bf16[128,768]{1,0:T(8,128)(2,1)S(1)}, bf16[128,768]{1,0:T(8,128)(2,1)S(1)}, bf16[768,1536]{1,0:T(8,128)(2,1)S(1)}, bf16[1536,768]{1,0:T(8,128)(2,1)S(1)}) custom-call(bf16[128,768]{1,0:T(8,128)(2,1)} %tok_ref.1, bf16[768,1536]{1,0:T(8,128)(2,1)} %win_ref.1, bf16[1536,768]{1,0:T(8,128)(2,1)} %wout_ref.1, f32[1,768]{1,0:T(1,128)} %reshape.11.gain_ref, ...), custom_call_target="tpu_custom_call" | custom-call | flops 14495514624 | bytes 12582912 | tf_op jit(solution)/shard_map/mlp_block/pallas_call | solution.py:503
  142.8 0.7 copy.13
  143.5 0.7 copy.14
  144.2 1.4 copy.15
  145.6 1.4 copy.16

commit v3 on v2

--- a/solution.py
+++ b/solution.py
@@ -18,8 +18,10 @@
 EIGHTH = QUARTER // 2
 SHARE = ROWS // 2
 PIECES = 4
-X_LAST = (1, 2)
-MAX_COPIES = 200
+X_LAST = (2, 3)
+MAX_COPIES = 220
+SUB = WIDTH // 2
+GROUPS = ((0, 128), (128, 256), (384, 256), (640, 256), (896, 128))
 
 norm_eps = 1e-06
 GRAD_SCALE = 1.0 / math.sqrt(8192)
@@ -56,7 +58,7 @@
 
 def kernel(
     tok_ref, win_ref, wout_ref, gain_ref, cot_ref,
-    mixed_ref, gin_ref, gwin_ref, gwout_ref,
+    mixed_ref, gin_ref, pieces_ref,
     winc, woutc, xf, cf, pf, rf, pb, rb, slopes, hid, ghid,
     branch, zf, gnorm, zb, stat_out, stat_in, totals, scaled,
     dw, anti, near, qsum, far, tok_buf, win_buf, wout_buf, ssem, rsem, lsem,
@@ -126,8 +128,8 @@
         buf = bufs[name]
         for copy in ring[name][k]:
             copy.wait_recv()
-        for r in (2 * k - 1, 2 * k) if k < 4 else (7,):
-            sib_copies[name][r] = send(buf.at[c, slot(r)], buf.at[c, slot(r)], sib)
+        rows = block(*GROUPS[k])
+        sib_copies[name][k] = send(buf.at[c, rows], buf.at[c, rows], sib)
 
     def ring_forward(name, k):
         buf = bufs[name]
@@ -173,106 +175,111 @@
         send(win_ref.at[:, lane_sib], winc.at[c], sib),
     ]
 
-    def partial_product(src, weights, dst, r, transposed):
-        rows = slot(r)
-        if transposed:
-            total = right_contract(src[0, rows], weights[0])
-            total += right_contract(src[1, rows], weights[1])
-        else:
-            total = dot(src[0, rows], weights[0]) + dot(src[1, rows], weights[1])
-        dst[rows, :] = total.astype(BF16)
+    def sub(part):
+        return pl.ds(part * SUB, SUB)
+
+    arrived = set()
+
+    def arrive(key, *waits):
+        if key not in arrived:
+            arrived.add(key)
+            for wait in waits:
+                wait()
 
     partial_copies = {"f": {}, "b": {}}
-
-    def send_partial(name, part, landing, r):
-        partial_copies[name][r] = send(
-            part.at[block(r * ROWS + (1 - xl) * SHARE, SHARE)],
-            landing.at[block(r * SHARE, SHARE)],
+    share_copies = {"f": {}, "b": {}}
+    whole_copies = {"f": {}, "b": {}}
+
+    def send_partial(name, part, landing, g, u):
+        start, count = GROUPS[g]
+        half = count // 2
+        partial_copies[name][g, u] = send(
+            part.at[block(start + (1 - xl) * half, half), sub(u)],
+            landing.at[block(start // 2, half), sub(u)],
             xn,
         )
 
-    def f1(r):
-        if r == 0:
-            local[3].wait()
-            weight_copies[1].wait_recv()
-        sib_copies["x"][r].wait_recv()
-        partial_product(xf, winc, pf, r, False)
-        send_partial("f", pf, rf, r)
-
-    def b1(r):
-        if r == 0:
-            local[2].wait()
-            weight_copies[0].wait_recv()
-        sib_copies["c"][r].wait_recv()
-        partial_product(cf, woutc, pb, r, True)
-        send_partial("b", pb, rb, r)
-
-    share_copies = {"f": {}, "b": {}}
-    whole_copies = {"f": {}, "b": {}}
-
-    def send_share(name, buf, r):
-        mine = buf.at[c, block(r * ROWS + xl * SHARE, SHARE)]
-        share_copies[name][r] = send(mine, mine, xn)
-
-    def f2(r):
-        partial_copies["f"][r].wait_recv()
+    def send_share(name, buf, g, u):
+        start, count = GROUPS[g]
+        half = count // 2
+        mine = buf.at[c, block(start + xl * half, half), sub(u)]
+        share_copies[name][g, u] = send(mine, mine, xn)
+
+    def f1(g, u):
+        arrive("win", local[3].wait, weight_copies[1].wait_recv)
+        arrive(("x", g), sib_copies["x"][g].wait_recv)
+        rows, cols = block(*GROUPS[g]), sub(u)
+        total = dot(xf[0, rows], winc[0, :, cols]) + dot(xf[1, rows], winc[1, :, cols])
+        pf[rows, cols] = total.astype(BF16)
+        send_partial("f", pf, rf, g, u)
+
+    def b1(g, u):
+        arrive("wout", local[2].wait, weight_copies[0].wait_recv)
+        arrive(("c", g), sib_copies["c"][g].wait_recv)
+        rows, cols = block(*GROUPS[g]), sub(u)
+        total = right_contract(cf[0, rows], woutc[0, cols, :])
+        total += right_contract(cf[1, rows], woutc[1, cols, :])
+        pb[rows, cols] = total.astype(BF16)
+        send_partial("b", pb, rb, g, u)
+
+    def f2(g, u):
+        partial_copies["f"][g, u].wait_recv()
+        start, count = GROUPS[g]
+        mine, landed = start + xl * (count // 2), start // 2
 
         def tile(n, carry):
-            k = n * 16
-            pre_act = pf[block(r * ROWS + xl * SHARE + k, 16), :].astype(F32)
-            pre_act += rf[block(r * SHARE + k, 16), :].astype(F32)
+            k = n * 32
+            pre_act = pf[block(mine + k, 32), sub(u)].astype(F32)
+            pre_act += rf[block(landed + k, 32), sub(u)].astype(F32)
             act, slope = gelu_pair(pre_act)
-            slopes[block(r * SHARE + k, 16), :] = slope
-            hid[c, block(r * ROWS + xl * SHARE + k, 16), :] = act.astype(BF16)
+            slopes[block(landed + k, 32), sub(u)] = slope
+            hid[c, block(mine + k, 32), sub(u)] = act.astype(BF16)
             return carry
 
-        lax.fori_loop(0, SHARE // 16, tile, 0)
-        send_share("f", hid, r)
-
-    def b2(r):
-        partial_copies["b"][r].wait_recv()
+        lax.fori_loop(0, count // 64, tile, 0)
+        send_share("f", hid, g, u)
+
+    def b2(g, u):
+        partial_copies["b"][g, u].wait_recv()
+        start, count = GROUPS[g]
+        mine, landed = start + xl * (count // 2), start // 2
 
         def tile(n, carry):
-            k = n * 16
-            grad = pb[block(r * ROWS + xl * SHARE + k, 16), :].astype(F32)
-            grad += rb[block(r * SHARE + k, 16), :].astype(F32)
-            grad *= slopes[block(r * SHARE + k, 16), :]
-            ghid[c, block(r * ROWS + xl * SHARE + k, 16), :] = grad.astype(BF16)
+            k = n * 32
+            grad = pb[block(mine + k, 32), sub(u)].astype(F32)
+            grad += rb[block(landed + k, 32), sub(u)].astype(F32)
+            grad *= slopes[block(landed + k, 32), sub(u)]
+            ghid[c, block(mine + k, 32), sub(u)] = grad.astype(BF16)
             return carry
 
-        lax.fori_loop(0, SHARE // 16, tile, 0)
-        send_share("b", ghid, r)
-
-    def third(name, buf, r):
-        share_copies[name][r].wait_recv()
-        whole = buf.at[c, slot(r)]
-        whole_copies[name][r] = send(whole, whole, sib)
-
-    def f3(r):
-        third("f", hid, r)
-
-    def b3(r):
-        third("b", ghid, r)
-
-    waited = {"f": False, "b": False}
-
-    def whole_wait(name):
-        waited[name] = True
-        for r in range(N_TOK):
-            whole_copies[name][r].wait_recv()
+        lax.fori_loop(0, count // 64, tile, 0)
+        send_share("b", ghid, g, u)
+
+    def third(name, buf, g, u):
+        share_copies[name][g, u].wait_recv()
+        whole = buf.at[c, block(*GROUPS[g]), sub(u)]
+        whole_copies[name][g, u] = send(whole, whole, sib)
+
+    def f3(g, u):
+        third("f", hid, g, u)
+
+    def b3(g, u):
+        third("b", ghid, g, u)
+
+    def whole_wait(name, u):
+        waits = [whole_copies[name][g, u].wait_recv for g in range(len(GROUPS))]
+        arrive((name, "whole", u), *waits)
 
     def product_rows(src, dst, i, transposed):
-        if not waited["b" if transposed else "f"]:
-            whole_wait("b" if transposed else "f")
+        for u in range(2):
+            whole_wait("b" if transposed else "f", u)
         rows = block(i * 256, 256)
         if transposed:
-            if i == 3:
-                local[5].wait()
+            arrive("win_buf", local[5].wait)
             total = right_contract(src[0, rows], win_buf[:, 0:WIDTH])
             total += right_contract(src[1, rows], win_buf[:, WIDTH : 2 * WIDTH])
         else:
-            if i == 3:
-                local[4].wait()
+            arrive("wout_buf", local[4].wait)
             total = dot(src[0, rows], wout_buf[0:WIDTH, :])
             total += dot(src[1, rows], wout_buf[WIDTH : 2 * WIDTH, :])
         dst[rows, :] = total.astype(BF16)
@@ -319,11 +326,15 @@
     qa, qb, qo = (y + 1) % N_Y, (y + N_Y - 1) % N_Y, (y + 2) % N_Y
 
     def weight_product(p):
-        if p < 2:
-            total = row_contract(hid[p], cf[c])
-        else:
-            total = row_contract(xf[c], ghid[p - 2])
-        dw[p] = (total * GRAD_SCALE).astype(BF16)
+        cols = sub(p % 2)
+        for core in range(2):
+            half = sub(core)
+            if p < 2:
+                total = row_contract(hid[core, :, cols], cf[c])
+                dw[p, half, :] = (total * GRAD_SCALE).astype(BF16)
+            else:
+                total = row_contract(xf[c], ghid[core, :, cols])
+                dw[p, :, half] = (total * GRAD_SCALE).astype(BF16)
 
     first_hop, second_hop, far_copies, spread, spread_on, across = {}, {}, {}, {}, {}, {}
     low, high = block(0, EIGHTH), block(EIGHTH, EIGHTH)
@@ -368,14 +379,8 @@
         else:
             far_copies[p] = send(qsum.at[p], far.at[p], xo)
 
-    def out_rows(p, start, size):
-        if p < 2:
-            return gwout_ref, (block(p * WIDTH + start, size), slice(None))
-        return gwin_ref, (block(start, size), pl.ds((p - 2) * WIDTH, WIDTH))
-
     def out_at(p, start, size):
-        ref, where = out_rows(p, start, size)
-        return ref.at[where]
+        return pieces_ref.at[p, block(start, size)]
 
     def r4(p):
         far_copies[p].wait_recv()
@@ -384,8 +389,7 @@
         def tile(n, carry):
             total = qsum[p, block(mine + n * 16, 16), :].astype(F32)
             total += far[p, block(n * 16, 16), :].astype(F32)
-            ref, where = out_rows(p, y * QUARTER + mine + n * 16, 16)
-            ref[where] = total.astype(BF16)
+            pieces_ref[p, block(y * QUARTER + mine + n * 16, 16), :] = total.astype(BF16)
             return carry
 
         lax.fori_loop(0, count // 16, tile, 0)
@@ -425,7 +429,7 @@
         row_rstd = lax.rsqrt(square_sum / D - row_mean * row_mean + norm_eps)
         totals[...] = jnp.where(lanes == 0, row_mean, row_rstd)
         centred = (tok_float - row_mean) * row_rstd
-        xf[c, slot(0)] = (centred * gain_ref[...]).astype(BF16)
+        xf[c, slot(0)] = (centred * gain_ref[...][None, :]).astype(BF16)
         start_ring("x", xf.at[c, slot(0)])
 
     def blk(name, i):
@@ -450,7 +454,7 @@
         return (tok_buf[...].astype(F32) - row_mean) * row_rstd, row_rstd
 
     def share_grad():
-        grad_scaled = ring_total("b", gnorm, zb) * gain_ref[...]
+        grad_scaled = ring_total("b", gnorm, zb) * gain_ref[...][None, :]
         scaled[...] = grad_scaled
         centred, _ = centred_rows()
         state["grad"] = share_stats(
@@ -468,28 +472,29 @@
         ).astype(BF16)
 
     def product(p):
-        if p in (0, 1) and not waited["f"]:
-            whole_wait("f")
-        if p in (2, 3) and not waited["b"]:
-            whole_wait("b")
+        whole_wait("f" if p < 2 else "b", p % 2)
         weight_product(p)
         r1(p)
 
     schedule = (
-        (b1, 0), (normalize,), (ring_wait, "c", 1), (f1, 0), (b1, 2), (f2, 0), (ring_wait, "x", 1), (f1, 2),
-        (ring_forward, "x", 1), (f1, 1), (f2, 2), (ring_wait, "x", 2), (ring_forward, "x", 2), (f2, 1),
-        (f1, 3), (ring_forward, "c", 1), (f1, 4), (ring_wait, "x", 3), (f2, 3), (f3, 1), (f1, 6), (f1, 5),
-        (f2, 4), (ring_wait, "c", 2), (ring_forward, "x", 3), (f3, 2), (ring_wait, "x", 4), (f3, 3),
-        (ring_forward, "c", 2), (f1, 7), (f2, 5), (f2, 7), (ring_wait, "c", 3), (f2, 6), (f3, 0), (b1, 3),
-        (f3, 7), (ring_forward, "c", 3), (f3, 4), (b2, 2), (f3, 5), (b2, 0), (f3, 6), (b1, 1), (blk, "f", 3),
-        (ring_wait, "c", 4), (b1, 6), (b1, 5), (b1, 4), (b2, 3), (product, 1), (b2, 1), (b3, 2), (r2, 1),
-        (b2, 6), (b1, 7), (blk, "f", 2), (product, 0), (r3, 1), (b2, 7), (b3, 3), (back_step, "f", 4),
-        (b3, 1), (b3, 6), (b2, 5), (b2, 4), (r2, 0), (b3, 0), (r4, 1), (b3, 5), (blk, "f", 1), (b3, 7),
-        (r3, 0), (r5, 1), (b3, 4), (product, 2), (r2, 2), (back_step, "f", 3), (blk, "f", 0), (blk, "b", 3),
-        (product, 3), (back_step, "f", 2), (blk, "b", 1), (r3, 2), (blk, "b", 2), (blk, "b", 0), (r2, 3),
-        (back_step, "b", 4), (r4, 2), (back_step, "b", 3), (r4, 0), (r3, 3), (back_step, "b", 2), (r5, 2),
-        (r4, 3), (r6, 1), (back_step, "b", 1), (r5, 0), (back_step, "f", 1), (r6, 2), (share_grad,), (r5, 3),
-        (finish_grad,), (finish_out,), (r6, 0), (r7, 2), (r7, 1), (r6, 3),
+        (normalize,), (b1, 0, 0), (b1, 0, 1), (ring_wait, "c", 1), (f1, 0, 1), (f1, 0, 0), (b1, 1, 1),
+        (ring_forward, "c", 1), (ring_wait, "x", 1), (f2, 0, 0), (f1, 1, 0), (f2, 0, 1),
+        (ring_forward, "x", 1), (f1, 1, 1), (f2, 1, 0), (ring_wait, "x", 2), (ring_wait, "c", 2), (f2, 1, 1),
+        (ring_forward, "x", 2), (f1, 2, 1), (f3, 1, 1), (b1, 1, 0), (f1, 2, 0), (ring_wait, "x", 3),
+        (ring_forward, "x", 3), (f1, 3, 0), (b2, 0, 0), (ring_wait, "x", 4), (f3, 0, 0), (f2, 2, 1),
+        (f2, 3, 0), (f3, 1, 0), (f1, 4, 0), (ring_forward, "c", 2), (f1, 3, 1), (f1, 4, 1),
+        (ring_wait, "c", 3), (b3, 0, 0), (ring_forward, "c", 3), (f2, 2, 0), (f3, 0, 1), (f2, 4, 0),
+        (f2, 4, 1), (ring_wait, "c", 4), (f2, 3, 1), (f3, 3, 0), (f3, 2, 0), (b1, 3, 1), (b2, 1, 0),
+        (f3, 4, 0), (product, 0), (b1, 2, 0), (f3, 3, 1), (f3, 4, 1), (b1, 4, 0), (b1, 3, 0), (b3, 1, 0),
+        (f3, 2, 1), (r2, 0), (product, 1), (b2, 0, 1), (b2, 4, 0), (b2, 3, 0), (b2, 2, 0), (b2, 1, 1),
+        (b3, 3, 0), (b1, 2, 1), (b3, 0, 1), (blk, "f", 3), (b2, 3, 1), (b3, 4, 0), (r2, 1), (b3, 2, 0),
+        (product, 2), (b1, 4, 1), (b2, 2, 1), (blk, "f", 0), (b2, 4, 1), (r3, 1), (b3, 3, 1), (b3, 1, 1),
+        (back_step, "f", 4), (r2, 2), (b3, 2, 1), (b3, 4, 1), (product, 3), (r3, 2), (blk, "b", 3),
+        (back_step, "b", 4), (r3, 0), (blk, "f", 1), (blk, "b", 1), (blk, "b", 2), (r2, 3), (blk, "f", 2),
+        (back_step, "f", 3), (back_step, "b", 3), (blk, "b", 0), (r4, 2), (r3, 3), (r5, 2),
+        (back_step, "f", 2), (r4, 1), (back_step, "f", 1), (r6, 2), (r4, 3), (r5, 1), (r5, 3), (finish_out,),
+        (back_step, "b", 2), (r4, 0), (back_step, "b", 1), (r6, 3), (r7, 2), (r5, 0), (share_grad,), (r6, 1),
+        (finish_grad,), (r6, 0), (r7, 3),
     )
     for step, *where in schedule:
         step(*where)
@@ -497,19 +502,37 @@
         copy.wait_send()
 
 
+def write_out(mixed_in, gin_in, pieces, mixed_ref, gin_ref, gwin_ref, gwout_ref, sems):
+    pairs = [(mixed_in, mixed_ref), (gin_in, gin_ref)]
+    for p in range(PIECES):
+        for core in range(2):
+            half = pl.ds(core * SUB, SUB)
+            place = pl.ds(core * WIDTH + (p % 2) * SUB, SUB)
+            if p < 2:
+                pairs.append((pieces.at[p, half, :], gwout_ref.at[place, :]))
+            else:
+                pairs.append((pieces.at[p, :, half], gwin_ref.at[:, place]))
+    copies = [
+        pltpu.make_async_copy(src, dst, sems.at[i]) for i, (src, dst) in enumerate(pairs)
+    ]
+    for copy in copies:
+        copy.start()
+    for copy in copies:
+        copy.wait()
+
+
 def shards(tokens, w_in, w_out, gain, cotangent):
     vmem = pl.BlockSpec(memory_space=pltpu.VMEM)
     anywhere = pl.BlockSpec(memory_space=pl.ANY)
-    return pl.pallas_call(
+    mixed, grad_input, pieces = pl.pallas_call(
         kernel,
         out_shape=(
             pltpu.VMEM((ROWS, WIDTH), BF16),
             pltpu.VMEM((ROWS, WIDTH), BF16),
-            pltpu.VMEM((WIDTH, 2 * WIDTH), BF16),
-            pltpu.VMEM((2 * WIDTH, WIDTH), BF16),
+            pltpu.VMEM((PIECES, WIDTH, WIDTH), BF16),
         ),
         in_specs=[anywhere, anywhere, anywhere, vmem, anywhere],
-        out_specs=(vmem,) * 4,
+        out_specs=(vmem,) * 3,
         scratch_shapes=[
             pltpu.VMEM((2, WIDTH, WIDTH), BF16),
             pltpu.VMEM((2, WIDTH, WIDTH), BF16),
@@ -549,7 +572,21 @@
             flops=6 * 2 * TOK * WIDTH * 2 * WIDTH, bytes_accessed=12 << 20, transcendentals=0
         ),
         name="mlp_block",
-    )(tokens, w_in, w_out, gain.reshape(1, WIDTH), cotangent)
+    )(tokens, w_in, w_out, gain, cotangent)
+    return pl.pallas_call(
+        write_out,
+        out_shape=(
+            jax.ShapeDtypeStruct((ROWS, WIDTH), BF16),
+            jax.ShapeDtypeStruct((ROWS, WIDTH), BF16),
+            jax.ShapeDtypeStruct((WIDTH, 2 * WIDTH), BF16),
+            jax.ShapeDtypeStruct((2 * WIDTH, WIDTH), BF16),
+        ),
+        in_specs=[anywhere] * 3,
+        out_specs=(anywhere,) * 4,
+        scratch_shapes=[pltpu.SemaphoreType.DMA((2 + 2 * PIECES,))],
+        compiler_params=pltpu.CompilerParams(vmem_limit_bytes=1 << 20),
+        name="write_out",
+    )(*(pltpu.with_memory_space_constraint(x, pltpu.VMEM) for x in (mixed, grad_input, pieces)))
 
 
 def solution(mesh):

time: 148 us -> 141 us (0.953)
  local copies, waits for them, and re-layouts: 5.43 us -> 0 us
    unnamed x4 -> x0, local copies, waits for them, and re-layouts: 4.17 us -> none
    pallas_call x1, Pallas kernels: 141 us -> 138 us  [shards(): pl.pallas_call(kernel, out_shape=(pltpu.VMEM((ROWS, WIDTH), BF16), pltpu....]
    pallas_call x0 -> x1, Pallas kernels: none -> 2.39 us  [shards(): pl.pallas_call(write_out, out_shape=(jax.ShapeDtypeStruct((ROWS, WIDTH),...]
where the time goes in v3:
time: 141 us
  Pallas kernels  140 us (99%)
    pallas_call x1, Pallas kernels, shards(): pl.pallas_call(kernel, out_shape=(pltpu.VMEM((ROWS, WIDTH), BF16), pltpu....  138 us

profile of v3, /device:TPU:1, one launch (start us, length us, event | category | flops | bytes accessed | tf_op | source)
XLA Modules:
  0.0 141.3 jit_solution(13455346048197573766)
XLA Ops:
  0.6 138.1 %mlp_block.1 = (bf16[128,768]{1,0:T(8,128)(2,1)S(1)}, bf16[128,768]{1,0:T(8,128)(2,1)S(1)}, bf16[4,768,768]{2,1,0:T(8,128)(2,1)S(1)}) custom-call(bf16[128,768]{1,0:T(8,128)(2,1)} %tok_ref.1, bf16[768,1536]{1,0:T(8,128)(2,1)} %win_ref.1, bf16[1536,768]{1,0:T(8,128)(2,1)} %wout_ref.1, f32[768]{0:T(1024)} %gain_ref.1, bf16[128,768]{1,0:T(8,128)(2,1)} %cot_ref.1), custom_call_target="tpu_custom_call" | custom-call | flops 14495514624 | bytes 12582912 | tf_op jit(solution)/shard_map/mlp_block/pallas_call | solution.py:527
  138.7 2.4 %write_out.1 = (bf16[128,768]{1,0:T(8,128)(2,1)}, bf16[128,768]{1,0:T(8,128)(2,1)}, bf16[768,1536]{1,0:T(8,128)(2,1)}, bf16[1536,768]{1,0:T(8,128)(2,1)}) custom-call(bf16[128,768]{1,0:T(8,128)(2,1)S(1)} %get-tuple-element.7.mixed_in, bf16[128,768]{1,0:T(8,128)(2,1)S(1)} %get-tuple-element.8.gin_in, bf16[4,768,768]{2,1,0:T(8,128)(2,1)S(1)} %get-tuple-element.9.pieces), custom_call_target="tpu_custom_call" | custom-call | tf_op jit(solution)/shard_map/write_out/pallas_call | solution.py:576

commit v4 on v3

--- a/solution.py
+++ b/solution.py
@@ -18,7 +18,7 @@
 EIGHTH = QUARTER // 2
 SHARE = ROWS // 2
 PIECES = 4
-X_LAST = (2, 3)
+X_LAST = (1,)
 MAX_COPIES = 220
 SUB = WIDTH // 2
 GROUPS = ((0, 128), (128, 256), (384, 256), (640, 256), (896, 128))
@@ -76,7 +76,6 @@
 
     own_half, sib_half = c * WIDTH, (1 - c) * WIDTH
     lane_own = pl.ds(pl.multiple_of(own_half, WIDTH), WIDTH)
-    lane_sib = pl.ds(pl.multiple_of(sib_half, WIDTH), WIDTH)
 
     barrier = pltpu.get_barrier_semaphore()
     for peer in peers:
@@ -170,10 +169,12 @@
     stats = share_stats(0, tok_sum, tok_squares)
     local[1].wait()
     start_ring("c", cf.at[c, slot(0)])
-    weight_copies = [
-        send(wout_ref.at[lane_sib, :], woutc.at[c], sib),
-        send(win_ref.at[:, lane_sib], winc.at[c], sib),
-    ]
+    weight_copies = {}
+    for u in range(2):
+        theirs = pl.ds(pl.multiple_of(sib_half + u * SUB, SUB), SUB)
+        here = pl.ds(u * SUB, SUB)
+        weight_copies["out", u] = send(wout_ref.at[theirs, :], woutc.at[c, here, :], sib)
+        weight_copies["in", u] = send(win_ref.at[:, theirs], winc.at[c, :, here], sib)
 
     def sub(part):
         return pl.ds(part * SUB, SUB)
@@ -206,7 +207,8 @@
         share_copies[name][g, u] = send(mine, mine, xn)
 
     def f1(g, u):
-        arrive("win", local[3].wait, weight_copies[1].wait_recv)
+        arrive("win", local[3].wait)
+        arrive(("in", u), weight_copies["in", u].wait_recv)
         arrive(("x", g), sib_copies["x"][g].wait_recv)
         rows, cols = block(*GROUPS[g]), sub(u)
         total = dot(xf[0, rows], winc[0, :, cols]) + dot(xf[1, rows], winc[1, :, cols])
@@ -214,7 +216,8 @@
         send_partial("f", pf, rf, g, u)
 
     def b1(g, u):
-        arrive("wout", local[2].wait, weight_copies[0].wait_recv)
+        arrive("wout", local[2].wait)
+        arrive(("out", u), weight_copies["out", u].wait_recv)
         arrive(("c", g), sib_copies["c"][g].wait_recv)
         rows, cols = block(*GROUPS[g]), sub(u)
         total = right_contract(cf[0, rows], woutc[0, cols, :])
@@ -477,24 +480,24 @@
         r1(p)
 
     schedule = (
-        (normalize,), (b1, 0, 0), (b1, 0, 1), (ring_wait, "c", 1), (f1, 0, 1), (f1, 0, 0), (b1, 1, 1),
-        (ring_forward, "c", 1), (ring_wait, "x", 1), (f2, 0, 0), (f1, 1, 0), (f2, 0, 1),
-        (ring_forward, "x", 1), (f1, 1, 1), (f2, 1, 0), (ring_wait, "x", 2), (ring_wait, "c", 2), (f2, 1, 1),
-        (ring_forward, "x", 2), (f1, 2, 1), (f3, 1, 1), (b1, 1, 0), (f1, 2, 0), (ring_wait, "x", 3),
-        (ring_forward, "x", 3), (f1, 3, 0), (b2, 0, 0), (ring_wait, "x", 4), (f3, 0, 0), (f2, 2, 1),
-        (f2, 3, 0), (f3, 1, 0), (f1, 4, 0), (ring_forward, "c", 2), (f1, 3, 1), (f1, 4, 1),
-        (ring_wait, "c", 3), (b3, 0, 0), (ring_forward, "c", 3), (f2, 2, 0), (f3, 0, 1), (f2, 4, 0),
-        (f2, 4, 1), (ring_wait, "c", 4), (f2, 3, 1), (f3, 3, 0), (f3, 2, 0), (b1, 3, 1), (b2, 1, 0),
-        (f3, 4, 0), (product, 0), (b1, 2, 0), (f3, 3, 1), (f3, 4, 1), (b1, 4, 0), (b1, 3, 0), (b3, 1, 0),
-        (f3, 2, 1), (r2, 0), (product, 1), (b2, 0, 1), (b2, 4, 0), (b2, 3, 0), (b2, 2, 0), (b2, 1, 1),
-        (b3, 3, 0), (b1, 2, 1), (b3, 0, 1), (blk, "f", 3), (b2, 3, 1), (b3, 4, 0), (r2, 1), (b3, 2, 0),
-        (product, 2), (b1, 4, 1), (b2, 2, 1), (blk, "f", 0), (b2, 4, 1), (r3, 1), (b3, 3, 1), (b3, 1, 1),
-        (back_step, "f", 4), (r2, 2), (b3, 2, 1), (b3, 4, 1), (product, 3), (r3, 2), (blk, "b", 3),
-        (back_step, "b", 4), (r3, 0), (blk, "f", 1), (blk, "b", 1), (blk, "b", 2), (r2, 3), (blk, "f", 2),
-        (back_step, "f", 3), (back_step, "b", 3), (blk, "b", 0), (r4, 2), (r3, 3), (r5, 2),
-        (back_step, "f", 2), (r4, 1), (back_step, "f", 1), (r6, 2), (r4, 3), (r5, 1), (r5, 3), (finish_out,),
-        (back_step, "b", 2), (r4, 0), (back_step, "b", 1), (r6, 3), (r7, 2), (r5, 0), (share_grad,), (r6, 1),
-        (finish_grad,), (r6, 0), (r7, 3),
+        (b1, 0, 0), (normalize,), (b1, 0, 1), (ring_wait, "c", 1), (f1, 0, 0), (f1, 0, 1), (b1, 1, 0),
+        (ring_wait, "x", 1), (ring_forward, "x", 1), (f2, 0, 1), (f2, 0, 0), (b2, 0, 0), (f1, 1, 0),
+        (f1, 1, 1), (ring_wait, "x", 2), (ring_forward, "x", 2), (f1, 2, 1), (ring_forward, "c", 1),
+        (f1, 2, 0), (f2, 1, 0), (f2, 2, 1), (ring_wait, "x", 3), (b3, 0, 0), (f1, 3, 0), (f1, 3, 1),
+        (ring_forward, "x", 3), (ring_wait, "c", 2), (ring_forward, "c", 2), (f3, 0, 1), (f2, 2, 0),
+        (f3, 1, 0), (ring_wait, "x", 4), (f1, 4, 0), (f2, 3, 0), (ring_wait, "c", 3), (f2, 4, 0),
+        (ring_forward, "c", 3), (f2, 3, 1), (f1, 4, 1), (f3, 2, 0), (f3, 3, 0), (f3, 0, 0), (b1, 2, 0),
+        (f3, 4, 0), (ring_wait, "c", 4), (product, 0), (f3, 3, 1), (f2, 4, 1), (b1, 4, 0), (f3, 2, 1),
+        (b2, 1, 0), (f3, 4, 1), (f2, 1, 1), (b1, 3, 0), (b2, 2, 0), (b1, 2, 1), (r2, 0), (f3, 1, 1),
+        (product, 1), (b2, 4, 0), (b2, 3, 0), (r3, 0), (blk, "f", 0), (b3, 2, 0), (b3, 1, 0), (b1, 1, 1),
+        (b3, 4, 0), (blk, "f", 2), (b2, 2, 1), (r2, 1), (blk, "f", 3), (b3, 3, 0), (product, 2), (b1, 3, 1),
+        (b1, 4, 1), (blk, "f", 1), (r4, 0), (b2, 1, 1), (b2, 3, 1), (back_step, "f", 4), (b2, 0, 1),
+        (b2, 4, 1), (r2, 2), (b3, 3, 1), (r5, 0), (b3, 1, 1), (b3, 2, 1), (r3, 1), (b3, 0, 1), (b3, 4, 1),
+        (product, 3), (back_step, "f", 3), (blk, "b", 3), (r3, 2), (r2, 3), (back_step, "b", 4), (r4, 1),
+        (blk, "b", 2), (back_step, "f", 2), (back_step, "b", 3), (r4, 2), (blk, "b", 0), (r3, 3),
+        (blk, "b", 1), (back_step, "b", 2), (r5, 1), (r4, 3), (r6, 0), (back_step, "b", 1),
+        (back_step, "f", 1), (r5, 2), (r6, 1), (share_grad,), (r5, 3), (finish_grad,), (finish_out,), (r6, 2),
+        (r7, 1), (r6, 3),
     )
     for step, *where in schedule:
         step(*where)

time: 141 us -> 139 us (0.986)
  Pallas kernels: 140 us -> 138 us
    pallas_call x1, Pallas kernels: 138 us -> 136 us  [shards(): pl.pallas_call(kernel, out_shape=(pltpu.VMEM((ROWS, WIDTH), BF16), pltpu....]
where the time goes in v4:
time: 139 us
  Pallas kernels  138 us (99%)
    pallas_call x1, Pallas kernels, shards(): pl.pallas_call(kernel, out_shape=(pltpu.VMEM((ROWS, WIDTH), BF16), pltpu....  136 us

profile of v4, /device:TPU:1, one launch (start us, length us, event | category | flops | bytes accessed | tf_op | source)
XLA Modules:
  0.0 138.9 jit_solution(18419751361031428970)
XLA Ops:
  0.6 135.7 %mlp_block.1 = (bf16[128,768]{1,0:T(8,128)(2,1)S(1)}, bf16[128,768]{1,0:T(8,128)(2,1)S(1)}, bf16[4,768,768]{2,1,0:T(8,128)(2,1)S(1)}) custom-call(bf16[128,768]{1,0:T(8,128)(2,1)} %tok_ref.1, bf16[768,1536]{1,0:T(8,128)(2,1)} %win_ref.1, bf16[1536,768]{1,0:T(8,128)(2,1)} %wout_ref.1, f32[768]{0:T(1024)} %gain_ref.1, bf16[128,768]{1,0:T(8,128)(2,1)} %cot_ref.1), custom_call_target="tpu_custom_call" | custom-call | flops 14495514624 | bytes 12582912 | tf_op jit(solution)/shard_map/mlp_block/pallas_call | solution.py:530
  136.3 2.4 %write_out.1 = (bf16[128,768]{1,0:T(8,128)(2,1)}, bf16[128,768]{1,0:T(8,128)(2,1)}, bf16[768,1536]{1,0:T(8,128)(2,1)}, bf16[1536,768]{1,0:T(8,128)(2,1)}) custom-call(bf16[128,768]{1,0:T(8,128)(2,1)S(1)} %get-tuple-element.7.mixed_in, bf16[128,768]{1,0:T(8,128)(2,1)S(1)} %get-tuple-element.8.gin_in, bf16[4,768,768]{2,1,0:T(8,128)(2,1)S(1)} %get-tuple-element.9.pieces), custom_call_target="tpu_custom_call" | custom-call | tf_op jit(solution)/shard_map/write_out/pallas_call | solution.py:579

commit v5 on v4

--- a/solution.py
+++ b/solution.py
@@ -14,12 +14,13 @@
 TOK = 1024
 N_TOK = 8
 N_Y = 4
-QUARTER = WIDTH // N_Y
+HALF = WIDTH // 2
+QUARTER = HALF // N_Y
 EIGHTH = QUARTER // 2
 SHARE = ROWS // 2
-PIECES = 4
-X_LAST = (1,)
-MAX_COPIES = 220
+PIECES = 8
+X_LAST = (2, 3)
+MAX_COPIES = 256
 SUB = WIDTH // 2
 GROUPS = ((0, 128), (128, 256), (384, 256), (640, 256), (896, 128))
 
@@ -334,10 +335,11 @@
             half = sub(core)
             if p < 2:
                 total = row_contract(hid[core, :, cols], cf[c])
-                dw[p, half, :] = (total * GRAD_SCALE).astype(BF16)
+                dw[2 * p + core] = (total * GRAD_SCALE).astype(BF16)
             else:
-                total = row_contract(xf[c], ghid[core, :, cols])
-                dw[p, :, half] = (total * GRAD_SCALE).astype(BF16)
+                total = (row_contract(xf[c], ghid[core, :, cols]) * GRAD_SCALE).astype(BF16)
+                dw[2 * p, :, half] = total[0:HALF]
+                dw[2 * p + 1, :, half] = total[HALF:WIDTH]
 
     first_hop, second_hop, far_copies, spread, spread_on, across = {}, {}, {}, {}, {}, {}
     low, high = block(0, EIGHTH), block(EIGHTH, EIGHTH)
@@ -404,9 +406,9 @@
     def r5(p):
         for copy in spread[p]:
             copy.wait_recv()
-        mine, half = (xh * EIGHTH, EIGHTH // 2) if p in X_LAST else (0, EIGHTH)
+        mine, half, rest = (xh * EIGHTH, 32, 16) if p in X_LAST else (0, EIGHTH, EIGHTH)
         behind = out_at(p, qb * QUARTER + mine, half)
-        ahead = out_at(p, qa * QUARTER + mine + half, half)
+        ahead = out_at(p, qa * QUARTER + mine + half, rest)
         spread_on[p] = (send(behind, behind, yp), send(ahead, ahead, ym))
         if p in X_LAST:
             for q in (qb, qa):
@@ -477,27 +479,29 @@
     def product(p):
         whole_wait("f" if p < 2 else "b", p % 2)
         weight_product(p)
-        r1(p)
+        r1(2 * p)
+        r1(2 * p + 1)
 
     schedule = (
-        (b1, 0, 0), (normalize,), (b1, 0, 1), (ring_wait, "c", 1), (f1, 0, 0), (f1, 0, 1), (b1, 1, 0),
-        (ring_wait, "x", 1), (ring_forward, "x", 1), (f2, 0, 1), (f2, 0, 0), (b2, 0, 0), (f1, 1, 0),
-        (f1, 1, 1), (ring_wait, "x", 2), (ring_forward, "x", 2), (f1, 2, 1), (ring_forward, "c", 1),
-        (f1, 2, 0), (f2, 1, 0), (f2, 2, 1), (ring_wait, "x", 3), (b3, 0, 0), (f1, 3, 0), (f1, 3, 1),
-        (ring_forward, "x", 3), (ring_wait, "c", 2), (ring_forward, "c", 2), (f3, 0, 1), (f2, 2, 0),
-        (f3, 1, 0), (ring_wait, "x", 4), (f1, 4, 0), (f2, 3, 0), (ring_wait, "c", 3), (f2, 4, 0),
-        (ring_forward, "c", 3), (f2, 3, 1), (f1, 4, 1), (f3, 2, 0), (f3, 3, 0), (f3, 0, 0), (b1, 2, 0),
-        (f3, 4, 0), (ring_wait, "c", 4), (product, 0), (f3, 3, 1), (f2, 4, 1), (b1, 4, 0), (f3, 2, 1),
-        (b2, 1, 0), (f3, 4, 1), (f2, 1, 1), (b1, 3, 0), (b2, 2, 0), (b1, 2, 1), (r2, 0), (f3, 1, 1),
-        (product, 1), (b2, 4, 0), (b2, 3, 0), (r3, 0), (blk, "f", 0), (b3, 2, 0), (b3, 1, 0), (b1, 1, 1),
-        (b3, 4, 0), (blk, "f", 2), (b2, 2, 1), (r2, 1), (blk, "f", 3), (b3, 3, 0), (product, 2), (b1, 3, 1),
-        (b1, 4, 1), (blk, "f", 1), (r4, 0), (b2, 1, 1), (b2, 3, 1), (back_step, "f", 4), (b2, 0, 1),
-        (b2, 4, 1), (r2, 2), (b3, 3, 1), (r5, 0), (b3, 1, 1), (b3, 2, 1), (r3, 1), (b3, 0, 1), (b3, 4, 1),
-        (product, 3), (back_step, "f", 3), (blk, "b", 3), (r3, 2), (r2, 3), (back_step, "b", 4), (r4, 1),
-        (blk, "b", 2), (back_step, "f", 2), (back_step, "b", 3), (r4, 2), (blk, "b", 0), (r3, 3),
-        (blk, "b", 1), (back_step, "b", 2), (r5, 1), (r4, 3), (r6, 0), (back_step, "b", 1),
-        (back_step, "f", 1), (r5, 2), (r6, 1), (share_grad,), (r5, 3), (finish_grad,), (finish_out,), (r6, 2),
-        (r7, 1), (r6, 3),
+        (b1, 0, 0), (normalize,), (b1, 0, 1), (f1, 0, 0), (ring_wait, "c", 1), (f1, 0, 1), (b1, 1, 0),
+        (ring_wait, "x", 1), (f2, 0, 1), (ring_forward, "x", 1), (f1, 1, 1), (f1, 1, 0), (b1, 1, 1),
+        (ring_wait, "x", 2), (ring_forward, "x", 2), (ring_forward, "c", 1), (f2, 0, 0), (f2, 1, 1),
+        (f1, 2, 0), (ring_wait, "x", 3), (f1, 2, 1), (ring_forward, "x", 3), (f1, 3, 1), (ring_wait, "c", 2),
+        (ring_forward, "c", 2), (f2, 2, 1), (ring_wait, "x", 4), (f1, 3, 0), (f1, 4, 0), (ring_wait, "c", 3),
+        (f3, 0, 1), (f1, 4, 1), (ring_forward, "c", 3), (f2, 3, 1), (f2, 4, 1), (f2, 2, 0), (f3, 0, 0),
+        (f3, 2, 1), (ring_wait, "c", 4), (f3, 1, 1), (f3, 3, 1), (f2, 3, 0), (f3, 4, 1), (f2, 1, 0),
+        (f2, 4, 0), (product, 1), (b1, 4, 0), (f3, 2, 0), (b1, 2, 0), (f3, 3, 0), (f3, 1, 0), (b1, 3, 0),
+        (f3, 4, 0), (b2, 0, 0), (product, 0), (blk, "f", 2), (b2, 1, 0), (r2, 0), (blk, "f", 3), (b3, 0, 0),
+        (b2, 3, 0), (b2, 2, 0), (r2, 1), (r2, 3), (b3, 1, 0), (b3, 3, 0), (b2, 4, 0), (r3, 0), (b1, 2, 1),
+        (r2, 2), (b3, 2, 0), (b1, 4, 1), (b3, 4, 0), (product, 2), (r4, 0), (r3, 1), (back_step, "f", 4),
+        (b2, 1, 1), (r2, 5), (b1, 3, 1), (back_step, "f", 3), (blk, "f", 1), (r3, 2), (b2, 2, 1), (r4, 1),
+        (b2, 0, 1), (back_step, "f", 2), (b2, 3, 1), (b2, 4, 1), (r5, 0), (r4, 2), (r3, 3), (r5, 1),
+        (b3, 0, 1), (b3, 2, 1), (r3, 5), (b3, 3, 1), (b3, 1, 1), (r2, 4), (r5, 2), (b3, 4, 1), (product, 3),
+        (blk, "f", 0), (r3, 4), (blk, "b", 3), (r6, 0), (back_step, "f", 1), (blk, "b", 1), (r2, 7),
+        (back_step, "b", 4), (r2, 6), (r4, 5), (blk, "b", 0), (blk, "b", 2), (back_step, "b", 3), (r4, 4),
+        (r3, 7), (r5, 5), (r3, 6), (r5, 4), (back_step, "b", 2), (r6, 2), (r4, 3), (finish_out,), (r4, 7),
+        (r5, 3), (r4, 6), (r6, 1), (r7, 2), (back_step, "b", 1), (r6, 3), (r5, 7), (r6, 5), (r5, 6), (r6, 4),
+        (share_grad,), (finish_grad,), (r6, 7), (r7, 3), (r6, 6),
     )
     for step, *where in schedule:
         step(*where)
@@ -508,13 +512,15 @@
 def write_out(mixed_in, gin_in, pieces, mixed_ref, gin_ref, gwin_ref, gwout_ref, sems):
     pairs = [(mixed_in, mixed_ref), (gin_in, gin_ref)]
     for p in range(PIECES):
-        for core in range(2):
-            half = pl.ds(core * SUB, SUB)
-            place = pl.ds(core * WIDTH + (p % 2) * SUB, SUB)
-            if p < 2:
-                pairs.append((pieces.at[p, half, :], gwout_ref.at[place, :]))
-            else:
-                pairs.append((pieces.at[p, :, half], gwin_ref.at[:, place]))
+        u, part = p // 2 % 2, p % 2
+        if p < PIECES // 2:
+            place = pl.ds(part * WIDTH + u * SUB, SUB)
+            pairs.append((pieces.at[p], gwout_ref.at[place, :]))
+        else:
+            for core in range(2):
+                place = pl.ds(core * WIDTH + u * SUB, SUB)
+                src = pieces.at[p, :, pl.ds(core * SUB, SUB)]
+                pairs.append((src, gwin_ref.at[pl.ds(part * HALF, HALF), place]))
     copies = [
         pltpu.make_async_copy(src, dst, sems.at[i]) for i, (src, dst) in enumerate(pairs)
     ]
@@ -532,7 +538,7 @@
         out_shape=(
             pltpu.VMEM((ROWS, WIDTH), BF16),
             pltpu.VMEM((ROWS, WIDTH), BF16),
-            pltpu.VMEM((PIECES, WIDTH, WIDTH), BF16),
+            pltpu.VMEM((PIECES, HALF, WIDTH), BF16),
         ),
         in_specs=[anywhere, anywhere, anywhere, vmem, anywhere],
         out_specs=(vmem,) * 3,
@@ -556,7 +562,7 @@
             pltpu.VMEM((2, 3, 8, ROWS), F32),
             pltpu.VMEM((ROWS, ROWS), F32),
             pltpu.VMEM((ROWS, WIDTH), F32),
-            pltpu.VMEM((PIECES, WIDTH, WIDTH), BF16),
+            pltpu.VMEM((PIECES, HALF, WIDTH), BF16),
             pltpu.VMEM((PIECES, QUARTER, WIDTH), BF16),
             pltpu.VMEM((PIECES, 2, QUARTER, WIDTH), BF16),
             pltpu.VMEM((PIECES, QUARTER, WIDTH), BF16),
@@ -586,7 +592,7 @@
         ),
         in_specs=[anywhere] * 3,
         out_specs=(anywhere,) * 4,
-        scratch_shapes=[pltpu.SemaphoreType.DMA((2 + 2 * PIECES,))],
+        scratch_shapes=[pltpu.SemaphoreType.DMA((2 + 3 * PIECES // 2,))],
         compiler_params=pltpu.CompilerParams(vmem_limit_bytes=1 << 20),
         name="write_out",
     )(*(pltpu.with_memory_space_constraint(x, pltpu.VMEM) for x in (mixed, grad_input, pieces)))

time: 139 us -> 144 us (1.036)
  Pallas kernels: 138 us -> 143 us
    pallas_call x1, Pallas kernels: 136 us -> 141 us  [shards(): pl.pallas_call(kernel, out_shape=(pltpu.VMEM((ROWS, WIDTH), BF16), pltpu....]
where the time goes in v5:
time: 144 us
  Pallas kernels  143 us (99%)
    pallas_call x1, Pallas kernels, shards(): pl.pallas_call(kernel, out_shape=(pltpu.VMEM((ROWS, WIDTH), BF16), pltpu....  141 us

profile of v5, /device:TPU:1, one launch (start us, length us, event | category | flops | bytes accessed | tf_op | source)
XLA Modules:
  0.0 144.2 jit_solution(17383664753384285121)
XLA Ops:
  0.6 141.0 %mlp_block.1 = (bf16[128,768]{1,0:T(8,128)(2,1)S(1)}, bf16[128,768]{1,0:T(8,128)(2,1)S(1)}, bf16[8,384,768]{2,1,0:T(8,128)(2,1)S(1)}) custom-call(bf16[128,768]{1,0:T(8,128)(2,1)} %tok_ref.1, bf16[768,1536]{1,0:T(8,128)(2,1)} %win_ref.1, bf16[1536,768]{1,0:T(8,128)(2,1)} %wout_ref.1, f32[768]{0:T(1024)} %gain_ref.1, bf16[128,768]{1,0:T(8,128)(2,1)} %cot_ref.1), custom_call_target="tpu_custom_call" | custom-call | flops 14495514624 | bytes 12582912 | tf_op jit(solution)/shard_map/mlp_block/pallas_call | solution.py:536
  141.6 2.4 %write_out.1 = (bf16[128,768]{1,0:T(8,128)(2,1)}, bf16[128,768]{1,0:T(8,128)(2,1)}, bf16[768,1536]{1,0:T(8,128)(2,1)}, bf16[1536,768]{1,0:T(8,128)(2,1)}) custom-call(bf16[128,768]{1,0:T(8,128)(2,1)S(1)} %get-tuple-element.7.mixed_in, bf16[128,768]{1,0:T(8,128)(2,1)S(1)} %get-tuple-element.8.gin_in, bf16[8,384,768]{2,1,0:T(8,128)(2,1)S(1)} %get-tuple-element.9.pieces), custom_call_target="tpu_custom_call" | custom-call | tf_op jit(solution)/shard_map/write_out/pallas_call | solution.py:585

commit v6 on v4

--- a/solution.py
+++ b/solution.py
@@ -480,24 +480,23 @@
         r1(p)
 
     schedule = (
-        (b1, 0, 0), (normalize,), (b1, 0, 1), (ring_wait, "c", 1), (f1, 0, 0), (f1, 0, 1), (b1, 1, 0),
-        (ring_wait, "x", 1), (ring_forward, "x", 1), (f2, 0, 1), (f2, 0, 0), (b2, 0, 0), (f1, 1, 0),
-        (f1, 1, 1), (ring_wait, "x", 2), (ring_forward, "x", 2), (f1, 2, 1), (ring_forward, "c", 1),
-        (f1, 2, 0), (f2, 1, 0), (f2, 2, 1), (ring_wait, "x", 3), (b3, 0, 0), (f1, 3, 0), (f1, 3, 1),
-        (ring_forward, "x", 3), (ring_wait, "c", 2), (ring_forward, "c", 2), (f3, 0, 1), (f2, 2, 0),
-        (f3, 1, 0), (ring_wait, "x", 4), (f1, 4, 0), (f2, 3, 0), (ring_wait, "c", 3), (f2, 4, 0),
-        (ring_forward, "c", 3), (f2, 3, 1), (f1, 4, 1), (f3, 2, 0), (f3, 3, 0), (f3, 0, 0), (b1, 2, 0),
-        (f3, 4, 0), (ring_wait, "c", 4), (product, 0), (f3, 3, 1), (f2, 4, 1), (b1, 4, 0), (f3, 2, 1),
-        (b2, 1, 0), (f3, 4, 1), (f2, 1, 1), (b1, 3, 0), (b2, 2, 0), (b1, 2, 1), (r2, 0), (f3, 1, 1),
-        (product, 1), (b2, 4, 0), (b2, 3, 0), (r3, 0), (blk, "f", 0), (b3, 2, 0), (b3, 1, 0), (b1, 1, 1),
-        (b3, 4, 0), (blk, "f", 2), (b2, 2, 1), (r2, 1), (blk, "f", 3), (b3, 3, 0), (product, 2), (b1, 3, 1),
-        (b1, 4, 1), (blk, "f", 1), (r4, 0), (b2, 1, 1), (b2, 3, 1), (back_step, "f", 4), (b2, 0, 1),
-        (b2, 4, 1), (r2, 2), (b3, 3, 1), (r5, 0), (b3, 1, 1), (b3, 2, 1), (r3, 1), (b3, 0, 1), (b3, 4, 1),
-        (product, 3), (back_step, "f", 3), (blk, "b", 3), (r3, 2), (r2, 3), (back_step, "b", 4), (r4, 1),
-        (blk, "b", 2), (back_step, "f", 2), (back_step, "b", 3), (r4, 2), (blk, "b", 0), (r3, 3),
-        (blk, "b", 1), (back_step, "b", 2), (r5, 1), (r4, 3), (r6, 0), (back_step, "b", 1),
-        (back_step, "f", 1), (r5, 2), (r6, 1), (share_grad,), (r5, 3), (finish_grad,), (finish_out,), (r6, 2),
-        (r7, 1), (r6, 3),
+        (normalize,), (b1, 0, 0), (b1, 0, 1), (f1, 0, 0), (ring_wait, "c", 1), (f1, 0, 1), (b1, 1, 0),
+        (ring_wait, "x", 1), (ring_forward, "x", 1), (f2, 0, 1), (f1, 1, 1), (b2, 0, 1), (f1, 1, 0),
+        (ring_wait, "x", 2), (f2, 0, 0), (ring_forward, "x", 2), (ring_forward, "c", 1), (f1, 2, 0),
+        (f1, 2, 1), (f2, 1, 0), (f2, 2, 0), (ring_wait, "x", 3), (ring_forward, "x", 3), (f1, 3, 0),
+        (f1, 3, 1), (ring_wait, "c", 2), (ring_forward, "c", 2), (ring_wait, "x", 4), (f3, 2, 0), (f1, 4, 0),
+        (f2, 3, 0), (f3, 0, 0), (f1, 4, 1), (ring_wait, "c", 3), (f2, 4, 0), (f2, 1, 1), (f3, 1, 0),
+        (ring_forward, "c", 3), (f3, 3, 0), (f2, 2, 1), (f2, 3, 1), (f3, 4, 0), (b2, 0, 0), (f2, 4, 1),
+        (ring_wait, "c", 4), (product, 0), (b3, 0, 1), (f3, 0, 1), (b1, 3, 0), (r2, 0), (f3, 4, 1),
+        (b1, 2, 0), (f3, 3, 1), (b3, 0, 0), (f3, 2, 1), (b2, 3, 0), (b1, 4, 0), (f3, 1, 1), (product, 1),
+        (b2, 1, 0), (blk, "f", 3), (b3, 3, 0), (blk, "f", 1), (b2, 2, 0), (b2, 4, 0), (back_step, "f", 4),
+        (blk, "f", 2), (r3, 0), (b3, 1, 0), (b1, 1, 1), (b1, 2, 1), (r2, 1), (b3, 2, 0), (b3, 4, 0),
+        (back_step, "f", 3), (product, 2), (r4, 0), (b1, 3, 1), (r2, 2), (b1, 4, 1), (b2, 2, 1), (b2, 3, 1),
+        (b3, 2, 1), (b2, 1, 1), (b2, 4, 1), (r3, 1), (r5, 0), (b3, 3, 1), (b3, 1, 1), (b3, 4, 1),
+        (product, 3), (r3, 2), (blk, "b", 3), (blk, "b", 2), (back_step, "b", 4), (blk, "f", 0), (r2, 3),
+        (r4, 1), (back_step, "f", 2), (blk, "b", 0), (r4, 2), (back_step, "b", 3), (blk, "b", 1), (r6, 0),
+        (r3, 3), (back_step, "f", 1), (r5, 1), (back_step, "b", 2), (r4, 3), (r5, 2), (back_step, "b", 1),
+        (r6, 1), (r5, 3), (finish_out,), (r6, 2), (r7, 1), (share_grad,), (finish_grad,), (r6, 3),
     )
     for step, *where in schedule:
         step(*where)
@@ -515,9 +514,12 @@
                 pairs.append((pieces.at[p, half, :], gwout_ref.at[place, :]))
             else:
                 pairs.append((pieces.at[p, :, half], gwin_ref.at[:, place]))
-    copies = [
-        pltpu.make_async_copy(src, dst, sems.at[i]) for i, (src, dst) in enumerate(pairs)
-    ]
+    copies = []
+    for src, dst in pairs:
+        rows = src.shape[0] // 2
+        for part in (pl.ds(0, rows), pl.ds(rows, rows)):
+            sem = sems.at[len(copies)]
+            copies.append(pltpu.make_async_copy(src.at[part, :], dst.at[part, :], sem))
     for copy in copies:
         copy.start()
     for copy in copies:
@@ -586,7 +588,7 @@
         ),
         in_specs=[anywhere] * 3,
         out_specs=(anywhere,) * 4,
-        scratch_shapes=[pltpu.SemaphoreType.DMA((2 + 2 * PIECES,))],
+        scratch_shapes=[pltpu.SemaphoreType.DMA((4 + 4 * PIECES,))],
         compiler_params=pltpu.CompilerParams(vmem_limit_bytes=1 << 20),
         name="write_out",
     )(*(pltpu.with_memory_space_constraint(x, pltpu.VMEM) for x in (mixed, grad_input, pieces)))

time: 139 us -> 140 us (level)
  Pallas kernels: 138 us -> 140 us
where the time goes in v6:
time: 140 us
  Pallas kernels  140 us (100%)
    pallas_call x1, Pallas kernels, shards(): pl.pallas_call(kernel, out_shape=(pltpu.VMEM((ROWS, WIDTH), BF16), pltpu....  137 us

profile of v6, /device:TPU:1, one launch (start us, length us, event | category | flops | bytes accessed | tf_op | source)
XLA Modules:
  0.0 140.3 jit_solution(11215265541442391730)
XLA Ops:
  0.6 137.1 %mlp_block.1 = (bf16[128,768]{1,0:T(8,128)(2,1)S(1)}, bf16[128,768]{1,0:T(8,128)(2,1)S(1)}, bf16[4,768,768]{2,1,0:T(8,128)(2,1)S(1)}) custom-call(bf16[128,768]{1,0:T(8,128)(2,1)} %tok_ref.1, bf16[768,1536]{1,0:T(8,128)(2,1)} %win_ref.1, bf16[1536,768]{1,0:T(8,128)(2,1)} %wout_ref.1, f32[768]{0:T(1024)} %gain_ref.1, bf16[128,768]{1,0:T(8,128)(2,1)} %cot_ref.1), custom_call_target="tpu_custom_call" | custom-call | flops 14495514624 | bytes 12582912 | tf_op jit(solution)/shard_map/mlp_block/pallas_call | solution.py:532
  137.7 2.5 %write_out.1 = (bf16[128,768]{1,0:T(8,128)(2,1)}, bf16[128,768]{1,0:T(8,128)(2,1)}, bf16[768,1536]{1,0:T(8,128)(2,1)}, bf16[1536,768]{1,0:T(8,128)(2,1)}) custom-call(bf16[128,768]{1,0:T(8,128)(2,1)S(1)} %get-tuple-element.7.mixed_in, bf16[128,768]{1,0:T(8,128)(2,1)S(1)} %get-tuple-element.8.gin_in, bf16[4,768,768]{2,1,0:T(8,128)(2,1)S(1)} %get-tuple-element.9.pieces), custom_call_target="tpu_custom_call" | custom-call | tf_op jit(solution)/shard_map/write_out/pallas_call | solution.py:581
